TPU v7x, 1024 devices: a whole 4x8x16 slice. The times are simulated.
1024 devices in a mesh: rep: 8 (over x, y_lo), exp: 32 (over z, core), node: 4 (over y_hi).
Axes of the slice: x: 4, y: 8 (y_hi: 4, y_lo: 2; y = y_hi * 2 + y_lo), z: 16, core: 2. Of those that a mesh axis runs over, the one named last changes fastest.
Arguments:
- grad_out: bfloat16 [16384, 1664], P(('exp', 'node')), may hold values from -4 to 4
- gates: float32 [16384, 2], P(('exp', 'node')), may hold values from 0.2 to 1
- expert_ids: int32 [16384, 2], P(('exp', 'node')), may hold values from 0 to 31, all different within a row
- saved_inputs: bfloat16 [32, 4, 320, 1664], P('exp', 'node'), may hold values from -6 to 6
- w_in: bfloat16 [32, 1664, 4096], P('exp', None, 'rep'), may hold values from -0.15625 to 0.15625
- w_out: bfloat16 [32, 1664, 4096], P('exp', None, 'rep'), may hold values from -0.09375 to 0.09375
Outputs:
- grad_inputs: bfloat16 [16384, 1664], P(('exp', 'node'), 'rep')
- grad_w_in: bfloat16 [32, 1664, 4096], P('exp', 'node', 'rep')
- grad_w_out: bfloat16 [32, 1664, 4096], P('exp', 'node', 'rep')
Inputs may be any that keep to these rules, and one draw needn't show every extreme that they name: `expert_ids`: each patch names 2 different experts, and every expert is named by some patch.
All inputs are finite; a program needn't handle non-finite values.
Results may differ from a plain program's by a relative error of at most 0.013.
Values may be sent and summed in bfloat16 or wider, within the bound.
No kernel may reach another device: no remote copies, remote signals or barrier semaphores. Data moves between devices by JAX's collectives and lax.ppermute only.
A program may use at most 64 MiB of HBM per device.

v0:
```python
import jax
import jax.numpy as jnp
from jax import lax
from jax.sharding import PartitionSpec as P

SQRT_HALF = 0.7071067811865476
INV_ROOT_TAU = 0.3989422804014327


def gelu_pair(hidden):
    cdf = 0.5 * (1.0 + lax.erf(hidden * SQRT_HALF))
    return (hidden * cdf, cdf + hidden * INV_ROOT_TAU * jnp.exp(-0.5 * hidden * hidden))


def slot_table(expert_ids, experts, slots):
    flat = expert_ids.T.reshape(-1)
    onehot = (flat[:, None] == jnp.arange(experts, dtype=jnp.int32)[None, :]).astype(jnp.int32)
    ranks = jnp.cumsum(onehot, axis=0) - onehot
    slot = jnp.sum(ranks * onehot, axis=1)
    return (flat, slot, slot < slots)


def local(grad_out, gates, expert_ids, saved_inputs, w_in, w_out):
    tok_here, width = grad_out.shape
    experts = lax.axis_size("exp")
    slots = saved_inputs.shape[2] // experts
    flat, slot, kept = slot_table(expert_ids, experts, slots)
    target = jnp.where(kept, flat * slots + slot, -1)
    places = jnp.arange(experts * slots, dtype=jnp.int32)
    match = target[None, :] == places[:, None]
    filled = jnp.any(match, axis=1)
    positions = jnp.arange(target.shape[0], dtype=jnp.int32)
    owner = jnp.sum(jnp.where(match, positions[None, :], 0), axis=1)
    token = owner % tok_here
    column = owner // tok_here
    scale = gates[token, column]
    outgoing = jnp.where(
        filled[:, None], scale[:, None] * grad_out[token].astype(jnp.float32), 0.0
    ).astype(jnp.bfloat16)
    arrived = lax.all_to_all(
        outgoing.reshape(experts, slots, width), "exp", split_axis=0, concat_axis=0, tiled=True
    )
    upstream = arrived.reshape(experts * slots, width)
    inputs = saved_inputs[0, 0]
    proj_in = w_in[0]
    proj_out = w_out[0]
    hidden = jnp.dot(inputs, proj_in, preferred_element_type=jnp.float32)
    act, slope = gelu_pair(hidden)
    act = act.astype(jnp.bfloat16)
    dact = jnp.dot(upstream, proj_out, preferred_element_type=jnp.float32)
    dhid = (dact * slope).astype(jnp.bfloat16)
    partial_value = lax.dot_general(
        dhid, proj_in, (((1,), (1,)), ((), ())), preferred_element_type=jnp.float32
    ).astype(jnp.bfloat16)
    grad_a = lax.dot_general(
        inputs, dhid, (((0,), (0,)), ((), ())), preferred_element_type=jnp.float32
    )
    grad_b = lax.dot_general(
        upstream, act, (((0,), (0,)), ((), ())), preferred_element_type=jnp.float32
    )
    summed = lax.psum_scatter(
        jnp.stack([grad_a, grad_b], axis=1).astype(jnp.bfloat16),
        "node",
        scatter_dimension=0,
        tiled=True,
    ).astype(jnp.float32)
    grad_w_in = summed[:, 0, :][None].astype(jnp.bfloat16)
    grad_w_out = summed[:, 1, :][None].astype(jnp.bfloat16)
    index = jnp.where(kept, flat * slots + slot, 0)
    back = lax.all_to_all(
        partial_value.reshape(experts, slots, width), "exp", split_axis=0, concat_axis=0, tiled=True
    )
    picked = back.reshape(experts * slots, width)[index].astype(jnp.float32)
    picked = jnp.where(kept[:, None], picked, 0.0)
    merged = jnp.sum(picked.reshape(-1, tok_here, width), axis=0)
    grad_inputs = lax.psum_scatter(merged, "rep", scatter_dimension=1, tiled=True)
    return (grad_inputs.astype(jnp.bfloat16), grad_w_in, grad_w_out)


def solution(mesh):
    return jax.shard_map(
        local,
        mesh=mesh,
        in_specs=(
            P(("exp", "node"), None),
            P(("exp", "node"), None),
            P(("exp", "node"), None),
            P("exp", "node", None, None),
            P("exp", None, "rep"),
            P("exp", None, "rep"),
        ),
        out_specs=(P(("exp", "node"), "rep"), P("exp", "node", "rep"), P("exp", "node", "rep")),
        check_vma=False,
    )
```

profile of v0, /device:TPU:1, one launch (start us, length us, event | category | flops | bytes accessed | tf_op | source)
XLA Modules:
  0.0 333.7 jit_solution(18142343894912660404)
XLA Ops:
  8.0 0.0 copy-start
  8.0 0.8 fusion.23
  8.8 0.6 reduce-window.6
  9.4 0.2 slice_reduce_fusion
  9.6 0.8 fusion.22
  10.4 0.7 add_select_fusion
  11.1 0.1 select_reduce_fusion
  11.2 0.2 fusion.19
  11.4 5.0 %gather_fusion.1 = bf16[320,1664]{1,0:T(8,128)(2,1)S(1)} fusion(bf16[128,1664]{1,0:T(8,128)(2,1)} %param.6, s32[1024]{0:T(1024)S(1)} %pad_clamp_fusion.1), kind=kCustom, calls=%fused_computation.1 | custom fusion | bytes 2131200 | tf_op jit(solution)/shard_map/gather | solution.py:38
  16.4 0.0 copy-start.1
  16.4 1.9 reshape.227
  18.3 0.0 copy-done.1
  18.3 3.1 gather_fusion
  21.4 0.1 mul.72
  21.5 0.1 broadcast_in_dim.58
  21.6 3.5 %select_convert_fusion = bf16[32,10,1664]{2,1,0:T(8,128)(2,1)} fusion(f32[32,10,1664]{2,1,0:T(8,128)} %reshape.227, f32[32,10]{1,0:T(8,128)S(1)} %mul.72, pred[32,10]{1,0:T(8,128)(4,1)S(1)} %broadcast_in_dim.58), kind=kLoop, calls=%fused_computation.4 | loop fusion | flops 1597440 | bytes 3196480 | tf_op jit(solution)/shard_map/convert_element_type | solution.py:39
  25.2 20.4 %all-to-all-start = ((bf16[32,10,1664]{2,1,0:T(8,128)(2,1)}), bf16[32,10,1664]{2,1,0:T(8,128)(2,1)S(1)}, u32[]{:S(2)}, u32[]{:S(2)}) async-start(bf16[32,10,1664]{2,1,0:T(8,128)(2,1)} %select_convert_fusion), calls=%async_computation | async-start | bytes 3407872 | tf_op jit(solution)/shard_map/all_to_all | solution.py:40
  45.6 0.0 copy-done
  45.6 2.8 fusion.4
  48.4 80.3 %all-to-all-done = bf16[32,10,1664]{2,1,0:T(8,128)(2,1)S(1)} async-done(((bf16[32,10,1664]{2,1,0:T(8,128)(2,1)}), bf16[32,10,1664]{2,1,0:T(8,128)(2,1)S(1)}, u32[]{:S(2)}, u32[]{:S(2)}) %all-to-all-start) | async-done | bytes 1064992 | tf_op jit(solution)/shard_map/all_to_all | solution.py:40
  128.7 1.2 reshape.224
  129.9 2.8 fusion.11
  132.7 0.8 convolution_convert_fusion.2
  133.5 1.4 reshape.225
  134.9 5.1 %all-to-all-start.1 = ((bf16[32,10,1664]{2,1,0:T(8,128)(2,1)}), bf16[32,10,1664]{2,1,0:T(8,128)(2,1)}, u32[]{:S(2)}, u32[]{:S(2)}) async-start(bf16[32,10,1664]{2,1,0:T(8,128)(2,1)} %reshape.225), calls=%async_computation.1 | async-start | bytes 3407872 | tf_op jit(solution)/shard_map/all_to_all | solution.py:70
  140.0 0.0 copy-start.2
  140.0 0.0 all-reduce.3.cloned.1.call-start
  140.1 0.0 copy-start.4
  140.1 2.5 fusion
  142.6 0.0 copy-done.2
  142.6 0.0 copy-done.4
  142.6 1.2 fusion.1
  143.7 2.1 pad_maximum_fusion
  145.8 9.3 %copy.34 = bf16[1664,2,512]{2,1,0:T(2,128)(2,1)} copy(bf16[1664,2,512]{0,2,1:T(8,128)(2,1)} %pad_maximum_fusion) | data formatting | bytes 6815744 | tf_op jit(solution)/shard_map/stack | solution.py:62
  155.1 0.0 copy-start.3
  155.1 0.0 all-reduce.3.cloned.1.call-update
  155.1 0.2 reduce-scatter.4.cloned.1.call-start
  155.4 0.4 copy-done.3
  155.8 67.8 %all-to-all-done.1 = bf16[32,10,1664]{2,1,0:T(8,128)(2,1)} async-done(((bf16[32,10,1664]{2,1,0:T(8,128)(2,1)}), bf16[32,10,1664]{2,1,0:T(8,128)(2,1)}, u32[]{:S(2)}, u32[]{:S(2)}) %all-to-all-start.1) | async-done | bytes 1064992 | tf_op jit(solution)/shard_map/all_to_all | solution.py:70
  223.6 1.7 reshape.226
  225.3 2.2 gather_fusion.2
  227.5 1.4 fusion.2
  229.0 1.2 copy.39
  230.2 0.0 reduce-scatter.4.cloned.1.call-update
  230.2 1.3 dynamic-slice
  232.1 88.5 %all-reduce.3.cloned.1.call-done = bf16[1664,2,512]{2,1,0:T(2,128)(2,1)} async-done(((bf16[1664,2,512]{2,1,0:T(2,128)(2,1)}), bf16[1664,2,512]{2,1,0:T(2,128)(2,1)}) %all-reduce.3.cloned.1.call-update) | async-done | bytes 3407888
  320.6 2.8 constant_dynamic-slice_fusion.1
  323.4 1.1 copy_bitcast_fusion
  324.5 0.0 reduce-scatter.4.cloned.1.call-done
  324.5 1.0 copy.40
  325.5 0.7 copy.37
  (8 shorter events, 0.1 us)
Async XLA Ops:
  8.0 37.6 %copy-start = (bf16[1,1664,512]{2,1,0:T(8,128)(2,1)S(1)}, bf16[1,1664,512]{2,1,0:T(8,128)(2,1)}, u32[]{:S(2)}) copy-start(bf16[1,1664,512]{2,1,0:T(8,128)(2,1)} %param.10) | copy-start | bytes 5111812
  16.4 1.9 copy-start.1
  25.2 103.5 %all-to-all-start = ((bf16[32,10,1664]{2,1,0:T(8,128)(2,1)}), bf16[32,10,1664]{2,1,0:T(8,128)(2,1)S(1)}, u32[]{:S(2)}, u32[]{:S(2)}) async-start(bf16[32,10,1664]{2,1,0:T(8,128)(2,1)} %select_convert_fusion), calls=%async_computation | async-start | bytes 3407872 | tf_op jit(solution)/shard_map/all_to_all | solution.py:40
  134.9 88.7 %all-to-all-start.1 = ((bf16[32,10,1664]{2,1,0:T(8,128)(2,1)}), bf16[32,10,1664]{2,1,0:T(8,128)(2,1)}, u32[]{:S(2)}, u32[]{:S(2)}) async-start(bf16[32,10,1664]{2,1,0:T(8,128)(2,1)} %reshape.225), calls=%async_computation.1 | async-start | bytes 3407872 | tf_op jit(solution)/shard_map/all_to_all | solution.py:70
  140.0 2.6 copy-start.2
  140.0 180.6 %all-reduce.3.cloned.1.call-start = ((), (), s32[]{:S(2)}) async-start(), calls=%async_computation.4 | async-start | bytes 6815744
  140.1 2.5 copy-start.4
  155.1 0.7 copy-start.3
  155.1 169.4 %reduce-scatter.4.cloned.1.call-start = ((), (), s32[]{:S(2)}) async-start(), calls=%async_computation.3 | async-start | bytes 958464
Sparse Core Ops, SparseCore 0:
  155.3 165.3 all-reduce.2
Sparse Core Ops, SparseCore 1:
  230.3 89.9 reduce-scatter.3
where the time goes:
time: 335 us; the launch traced here: 334 us
  waiting for transfers between devices  237 us (71%)
  local copies, waits for them, and re-layouts  34.7 us (10%)
  starting transfers between devices  25.8 us (8%)
  between operations  16.3 us (5%)
  other arithmetic  10.4 us (3%)
  matrix products  10 us (3%)
    unnamed x4, waiting for transfers between devices  88.5 us
    all_to_all x1, waiting for transfers between devices, local(): lax.all_to_all(outgoing.reshape(experts, slots, width), 'exp', split_axis...  80.3 us
    all_to_all x1, waiting for transfers between devices, local(): lax.all_to_all(partial_value.reshape(experts, slots, width), 'exp', split...  67.8 us
    all_to_all x1, starting transfers between devices, local(): lax.all_to_all(outgoing.reshape(experts, slots, width), 'exp', split_axis...  20.4 us
    another operation x1, local copies, waits for them, and re-layouts, local(): jnp.stack([grad_a, grad_b], axis=1).astype(jnp.bfloat16)  9.28 us
  transfers between devices with their start and end apart: 4, of which 3 were waited for; matrix products, arithmetic and copies ran while one was open for 9% of the time, Pallas kernels for 0%

commit v1 on v0

v1 whole, which is shorter than its diff:
```python
import jax
import jax.numpy as jnp
from jax import lax
from jax.experimental import pallas as pl
from jax.experimental.pallas import tpu as pltpu
from jax.sharding import PartitionSpec as P

SQRT_HALF = 0.7071067811865476
INV_ROOT_TAU = 0.3989422804014327

REP, EXP, NODE = 8, 32, 4
TOK, WIDTH, CAP = 128, 1664, 10
SLOTS = EXP * CAP
HID = 512
LANES = 128
TILES = WIDTH // LANES
COLS = WIDTH // REP
ROWS = WIDTH // NODE
SENDS = EXP // REP
PACKED = 136
BACK = 24
SHARE = SENDS * CAP

VMEM = pl.BlockSpec(memory_space=pltpu.VMEM)
SMEM = pl.BlockSpec(memory_space=pltpu.SMEM)
PARAMS = pltpu.CompilerParams(vmem_limit_bytes=48 * 1024 * 1024)


def iota(shape, dim):
    return lax.broadcasted_iota(jnp.int32, shape, dim)


def hot(mask):
    return jnp.where(mask, 1.0, 0.0).astype(jnp.bfloat16)


def dot(a, b, dims=((1,), (0,))):
    return lax.dot_general(a, b, (dims, ((), ())), preferred_element_type=jnp.float32)


def dispatch_kernel(pos_ref, ids_ref, gates_ref, grad_ref, o0, o1, o2, o3, code_ref):
    rep, src = pos_ref[0], pos_ref[1]
    lane = iota((TOK, LANES), 1)
    before = hot(iota((TOK, TOK), 0) > iota((TOK, TOK), 1))
    first = ids_ref[:, 0:1]
    second = ids_ref[:, 1:2]
    hot0 = hot(first == lane)
    hot1 = hot(second == lane)
    count0 = jnp.sum(hot0.astype(jnp.float32), axis=0, keepdims=True)
    rank0 = dot(before, hot0)
    rank1 = dot(before, hot1) + count0
    slot0 = jnp.sum(rank0 * hot0.astype(jnp.float32), axis=1, keepdims=True).astype(jnp.int32)
    slot1 = jnp.sum(rank1 * hot1.astype(jnp.float32), axis=1, keepdims=True).astype(jnp.int32)
    kept0 = slot0 < CAP
    kept1 = slot1 < CAP
    code_ref[:, 0:1] = jnp.where(kept0, first * BACK + slot0, -100)
    code_ref[:, 1:2] = jnp.where(kept1, second * BACK + slot1, -100)
    target0 = jnp.where(kept0, first * 16 + slot0, -1)
    target1 = jnp.where(kept1, second * 16 + slot1, -1)
    col = iota((1, LANES), 1)
    k = col >> 4
    c = col & 15
    expert = ((rep - src) & 7) + 8 * (((src >> 3) + k) & 3)
    wanted = jnp.where((c < CAP) & (k < SENDS), expert * 16 + c, -2)
    grad = grad_ref[...].astype(jnp.float32)
    scaled0 = (gates_ref[:, 0:1] * grad).astype(jnp.bfloat16)
    scaled1 = (gates_ref[:, 1:2] * grad).astype(jnp.bfloat16)
    rows = dot(hot(target0 == wanted), scaled0, ((0,), (0,))) + dot(
        hot(target1 == wanted), scaled1, ((0,), (0,))
    )
    rows = rows.astype(jnp.bfloat16)
    stacked = jnp.concatenate(
        [
            jnp.concatenate(
                [rows[16 * q : 16 * q + 16, LANES * t : LANES * (t + 1)] for q in range(SENDS)],
                axis=1,
            )
            for t in range(TILES)
        ],
        axis=0,
    )
    i = iota((PACKED, 16 * TILES), 1)
    squeeze = hot((iota((PACKED, 16 * TILES), 0) == (i >> 4) * CAP + (i & 15)) & ((i & 15) < CAP))
    packed = dot(squeeze, stacked).astype(jnp.bfloat16)
    for q, out in enumerate((o0, o1, o2, o3)):
        out[...] = packed[:, LANES * q : LANES * (q + 1)]


def unpack_kernel(i0, i1, i2, i3, out_ref):
    packed = jnp.concatenate([ref[...] for ref in (i0, i1, i2, i3)], axis=1)
    i = iota((16 * TILES, PACKED), 0)
    spread = hot((iota((16 * TILES, PACKED), 1) == (i >> 4) * CAP + (i & 15)) & ((i & 15) < CAP))
    stacked = dot(spread, packed).astype(jnp.bfloat16)
    rows = jnp.concatenate(
        [
            jnp.concatenate(
                [stacked[16 * t : 16 * t + 16, LANES * q : LANES * (q + 1)] for t in range(TILES)],
                axis=1,
            )
            for q in range(SENDS)
        ],
        axis=0,
    )
    j = iota((SHARE, 16 * SENDS), 0)
    k = lax.div(j, CAP)
    dense = hot(iota((SHARE, 16 * SENDS), 1) == k * 16 + (j - k * CAP))
    share = dot(dense, rows).astype(jnp.bfloat16)
    for q in range(REP):
        out_ref[q] = share


def middle_kernel(pos_ref, got_ref, w_in_ref, w_out_ref, slope_ref, up_ref, dhid_ref, part_ref):
    exp = pos_ref[1]
    j = iota((1, SLOTS), 1)
    block = lax.div(j, SHARE)
    rest = j - block * SHARE
    k = lax.div(rest, CAP)
    source = ((block - exp) & 7) + 8 * (((exp >> 3) - k) & 3)
    place = source * CAP + (rest - k * CAP)
    up = dot(hot(iota((SLOTS, SLOTS), 0) == place), got_ref[...]).astype(jnp.bfloat16)
    up_ref[...] = up
    dhid = (dot(up, w_out_ref[...]) * slope_ref[...]).astype(jnp.bfloat16)
    for q in range(NODE):
        dhid_ref[q] = dhid
    for q in range(REP):
        part_ref[q] = dot(dhid, w_in_ref[COLS * q : COLS * (q + 1), :], ((1,), (1,))).astype(
            jnp.bfloat16
        )


def back_kernel(part_ref, out_ref):
    total = part_ref[0].astype(jnp.float32)
    for q in range(1, REP):
        total = total + part_ref[q].astype(jnp.float32)
    total = total.astype(jnp.bfloat16)
    tail = dot(total, hot(iota((COLS, LANES), 0) == iota((COLS, LANES), 1) + LANES))
    m = iota((EXP * BACK, SLOTS), 0)
    s = lax.div(m, BACK)
    q = m - s * BACK
    j = iota((EXP * BACK, SLOTS), 1)
    one = hot((j == s * CAP + q) & (q < CAP))
    two = hot((j == s * CAP + q - CAP) & (q >= CAP) & (q < 2 * CAP))
    out = dot(one, total[:, :LANES]) + dot(two, tail.astype(jnp.bfloat16))
    out_ref[...] = out.astype(jnp.bfloat16)


def combine_kernel(code_ref, back_ref, out_ref):
    lane = iota((TOK, EXP * BACK), 1)
    code0 = code_ref[:, 0:1]
    code1 = code_ref[:, 1:2]
    back = back_ref[...]
    head = dot(hot((lane == code0) | (lane == code1)), back)
    tail = dot(hot((lane == code0 + CAP) | (lane == code1 + CAP)), back)
    out_ref[:, :LANES] = head.astype(jnp.bfloat16)
    out_ref[:, LANES:] = tail[:, : COLS - LANES].astype(jnp.bfloat16)


def call(kernel, out, in_specs, *args):
    return pl.pallas_call(
        kernel,
        out_shape=out,
        in_specs=in_specs,
        out_specs=jax.tree.map(lambda _: VMEM, out),
        compiler_params=PARAMS,
    )(*args)


def shape(*dims, dtype=jnp.bfloat16):
    return jax.ShapeDtypeStruct(dims, dtype)


def send_pairs(k):
    pairs = []
    for rep in range(REP):
        for src in range(EXP):
            dst = (rep - src) % 8 + 8 * ((src // 8 + k) % SENDS)
            pairs.append((rep * EXP + src, rep * EXP + dst))
    return pairs


def local(grad_out, gates, expert_ids, saved_inputs, w_in, w_out):
    pos = jnp.stack([lax.axis_index("rep"), lax.axis_index("exp")]).astype(jnp.int32)
    inputs = saved_inputs[0, 0]
    proj_in = w_in[0]
    proj_out = w_out[0]

    *packed, code = call(
        dispatch_kernel,
        [shape(PACKED, LANES)] * SENDS + [shape(TOK, 2, dtype=jnp.int32)],
        [SMEM] + [VMEM] * 3,
        pos,
        expert_ids,
        gates,
        grad_out,
    )
    landed = [lax.ppermute(p, ("rep", "exp"), send_pairs(k)) for k, p in enumerate(packed)]

    hidden = dot(inputs, proj_in)
    cdf = 0.5 * (1.0 + lax.erf(hidden * SQRT_HALF))
    act = (hidden * cdf).astype(jnp.bfloat16)
    slope = cdf + hidden * INV_ROOT_TAU * jnp.exp(-0.5 * hidden * hidden)
    input_cols = lax.all_to_all(
        inputs.reshape(SLOTS, NODE, ROWS).transpose(1, 0, 2), "node", 0, 0, tiled=True
    )

    shares = call(unpack_kernel, shape(REP, SHARE, WIDTH), [VMEM] * SENDS, *landed)
    got = lax.all_to_all(shares, "rep", 0, 0, tiled=True).reshape(SLOTS, WIDTH)
    up, dhid, part = call(
        middle_kernel,
        [shape(SLOTS, WIDTH), shape(NODE, SLOTS, HID), shape(REP, SLOTS, COLS)],
        [SMEM] + [VMEM] * 4,
        pos,
        got,
        proj_in,
        proj_out,
        slope,
    )
    part = lax.all_to_all(part, "rep", 0, 0, tiled=True)
    dhid_all = lax.all_to_all(dhid, "node", 0, 0, tiled=True)
    grad_b = dot(up, act, ((0,), (0,))).astype(jnp.bfloat16)
    grad_w_out = lax.psum_scatter(grad_b, "node", scatter_dimension=0, tiled=True)

    back = call(back_kernel, shape(EXP * BACK, LANES), [VMEM], part)
    back = lax.all_to_all(back.reshape(EXP, BACK, LANES), "exp", 0, 0, tiled=True)
    grad_inputs = call(
        combine_kernel, shape(TOK, COLS), [VMEM] * 2, code, back.reshape(EXP * BACK, LANES)
    )
    grad_w_in = dot(
        input_cols.reshape(NODE * SLOTS, ROWS), dhid_all.reshape(NODE * SLOTS, HID), ((0,), (0,))
    ).astype(jnp.bfloat16)
    return grad_inputs, grad_w_in[None], grad_w_out[None]


def solution(mesh):
    return jax.shard_map(
        local,
        mesh=mesh,
        in_specs=(
            P(("exp", "node"), None),
            P(("exp", "node"), None),
            P(("exp", "node"), None),
            P("exp", "node", None, None),
            P("exp", None, "rep"),
            P("exp", None, "rep"),
        ),
        out_specs=(P(("exp", "node"), "rep"), P("exp", "node", "rep"), P("exp", "node", "rep")),
        check_vma=False,
    )
```

time: 335 us -> 228 us (0.68)
  waiting for transfers between devices: 237 us -> 128 us
  starting transfers between devices: 25.8 us -> 60.8 us
  local copies, waits for them, and re-layouts: 34.7 us -> 7.11 us
  other arithmetic: 10.4 us -> 0.07 us
  Pallas kernels: 0 us -> 9.26 us
    unnamed x4 -> x1, waiting for transfers between devices: 88.5 us -> 0.02 us
    ppermute x0 -> x4, starting transfers between devices: none -> 31.3 us  [local(): lax.ppermute(p, ('rep', 'exp'), send_pairs(k))]
    all_to_all x2 -> x5, waiting for transfers between devices: 148 us -> 119 us  [the longest x1 53.6 us: local(): dhid_all = lax.all_to_all(dhid, 'node', 0, 0, tiled=True)]
    gather x3 -> x0, local copies, waits for them, and re-layouts: 10.3 us -> none  [the longest x1 4.98 us: local(): grad_out[token].astype(jnp.float32)]
    another operation x2 -> x0, local copies, waits for them, and re-layouts: 9.28 us -> none  [the longest x1 9.28 us: local(): jnp.stack([grad_a, grad_b], axis=1).astype(jnp.bfloat16)]
    pallas_call x0 -> x5, Pallas kernels: none -> 9.26 us  [call(): pl.pallas_call(kernel, out_shape=out, in_specs=in_specs, out_specs=jax.tr...]
    ppermute x0 -> x4, waiting for transfers between devices: none -> 8.8 us  [local(): lax.ppermute(p, ('rep', 'exp'), send_pairs(k))]
    convert_element_type x2 -> x0, other arithmetic: 4.36 us -> none  [the longest x1 3.55 us: local(): outgoing = jnp.where(filled[:, None], scale[:, None] * grad_out[token].as...]
  transfers between devices with their start and end apart: 4 -> 10, of which waited for: 3 -> 6; matrix products, arithmetic and copies ran while one was open for 9% -> 6% of each run, Pallas kernels for 0% -> 3%
where the time goes in v1:
time: 228 us
  waiting for transfers between devices  128 us (56%)
  starting transfers between devices  60.8 us (27%)
  between operations  14.1 us (6%)
  Pallas kernels  9.26 us (4%)
  matrix products  8.42 us (4%)
  local copies, waits for them, and re-layouts  7.11 us (3%)
    all_to_all x1, waiting for transfers between devices, local(): dhid_all = lax.all_to_all(dhid, 'node', 0, 0, tiled=True)  53.6 us
    ppermute x4, starting transfers between devices, local(): lax.ppermute(p, ('rep', 'exp'), send_pairs(k))  31.3 us
    all_to_all x1, waiting for transfers between devices, local(): lax.all_to_all(inputs.reshape(SLOTS, NODE, ROWS).transpose(1, 0, 2), 'nod...  21.7 us
    all_to_all x1, waiting for transfers between devices, local(): lax.all_to_all(back.reshape(EXP, BACK, LANES), 'exp', 0, 0, tiled=True)  15.4 us
    all_to_all x1, waiting for transfers between devices, local(): got = lax.all_to_all(shares, 'rep', 0, 0, tiled=True).reshape(SLOTS, WIDTH)  14.5 us
    all_to_all x1, waiting for transfers between devices, local(): part = lax.all_to_all(part, 'rep', 0, 0, tiled=True)  13.8 us
    pallas_call x5, Pallas kernels, call(): pl.pallas_call(kernel, out_shape=out, in_specs=in_specs, out_specs=jax.tr...  9.26 us
    ppermute x4, waiting for transfers between devices, local(): lax.ppermute(p, ('rep', 'exp'), send_pairs(k))  8.8 us
  transfers between devices with their start and end apart: 10, of which 6 were waited for; matrix products, arithmetic and copies ran while one was open for 6% of the time, Pallas kernels for 3%

profile of v1, /device:TPU:1, one launch (start us, length us, event | category | flops | bytes accessed | tf_op | source)
XLA Modules:
  0.0 227.7 jit_solution(4998724372861975286)
XLA Ops:
  7.2 0.8 copy.13.ids_ref
  8.0 0.8 copy.14.gates_ref
  8.7 0.1 pad_add_fusion.pos_ref
  8.8 0.0 copy-start
  8.8 1.0 copy-done
  9.8 1.6 shard_map.85
  11.4 8.4 %collective-permute-start = (bf16[136,128]{1,0:T(8,128)(2,1)S(1)}, bf16[136,128]{1,0:T(8,128)(2,1)S(1)}, u32[]{:S(2)}, u32[]{:S(2)}) collective-permute-start(bf16[136,128]{1,0:T(8,128)(2,1)S(1)} %get-tuple-element.12), channel_id=1, source_target_pairs={{0,0},{4,28},{8,24},{12,20},{16,16},{20,12},{24,8},{28,4},{32,32},... | collective-permute-start | bytes 104456 | tf_op jit(solution)/shard_map/ppermute | solution.py:196
  19.9 10.4 %collective-permute-start.1 = (bf16[136,128]{1,0:T(8,128)(2,1)S(1)}, bf16[136,128]{1,0:T(8,128)(2,1)S(1)}, u32[]{:S(2)}, u32[]{:S(2)}) collective-permute-start(bf16[136,128]{1,0:T(8,128)(2,1)S(1)} %get-tuple-element.13), channel_id=1, source_target_pairs={{0,32},{4,60},{8,56},{12,52},{16,48},{20,44},{24,40},{28,36},{32,6... | collective-permute-start | bytes 104456 | tf_op jit(solution)/shard_map/ppermute | solution.py:196
  30.3 9.2 %collective-permute-start.2 = (bf16[136,128]{1,0:T(8,128)(2,1)S(1)}, bf16[136,128]{1,0:T(8,128)(2,1)S(1)}, u32[]{:S(2)}, u32[]{:S(2)}) collective-permute-start(bf16[136,128]{1,0:T(8,128)(2,1)S(1)} %get-tuple-element.14), channel_id=1, source_target_pairs={{0,64},{4,92},{8,88},{12,84},{16,80},{20,76},{24,72},{28,68},{32,9... | collective-permute-start | bytes 104456 | tf_op jit(solution)/shard_map/ppermute | solution.py:196
  39.4 3.3 %collective-permute-start.3 = (bf16[136,128]{1,0:T(8,128)(2,1)S(1)}, bf16[136,128]{1,0:T(8,128)(2,1)S(1)}, u32[]{:S(2)}, u32[]{:S(2)}) collective-permute-start(bf16[136,128]{1,0:T(8,128)(2,1)S(1)} %get-tuple-element.15), channel_id=1, source_target_pairs={{0,96},{4,124},{8,120},{12,116},{16,112},{20,108},{24,104},{28,100... | collective-permute-start | bytes 104456 | tf_op jit(solution)/shard_map/ppermute | solution.py:196
  42.8 0.0 collective-permute-done.i0
  42.8 0.0 collective-permute-done.1.i1
  42.8 0.0 collective-permute-done.2.i2
  42.8 8.8 %collective-permute-done.3.i3 = bf16[136,128]{1,0:T(8,128)(2,1)S(1)} collective-permute-done((bf16[136,128]{1,0:T(8,128)(2,1)S(1)}, bf16[136,128]{1,0:T(8,128)(2,1)S(1)}, u32[]{:S(2)}, u32[]{:S(2)}) %collective-permute-start.3) | collective-permute-done | bytes 34848 | tf_op jit(solution)/shard_map/ppermute | solution.py:196
  51.6 1.4 shard_map.86
  53.0 0.0 copy-start.2
  53.0 6.0 %all-to-all-start = ((bf16[8,40,1664]{2,1,0:T(8,128)(2,1)}), bf16[8,40,1664]{2,1,0:T(8,128)(2,1)S(1)}, u32[]{:S(2)}, u32[]{:S(2)}) async-start(bf16[8,40,1664]{2,1,0:T(8,128)(2,1)} %shard_map.86), calls=%async_computation | async-start | bytes 2129920 | tf_op jit(solution)/shard_map/all_to_all | solution.py:207
  58.9 0.0 copy-done.2
  58.9 1.6 copy.17
  60.5 14.5 %all-to-all-done = bf16[8,40,1664]{2,1,0:T(8,128)(2,1)S(1)} async-done(((bf16[8,40,1664]{2,1,0:T(8,128)(2,1)}), bf16[8,40,1664]{2,1,0:T(8,128)(2,1)S(1)}, u32[]{:S(2)}, u32[]{:S(2)}) %all-to-all-start) | async-done | bytes 1064992 | tf_op jit(solution)/shard_map/all_to_all | solution.py:207
  75.0 0.0 copy-start.1
  75.0 5.0 %all-to-all-start.4 = ((bf16[4,320,416]{1,2,0:T(8,128)(2,1)}), bf16[4,320,416]{1,2,0:T(8,128)(2,1)}, u32[]{:S(2)}, u32[]{:S(2)}) async-start(bf16[4,320,416]{1,2,0:T(8,128)(2,1)} %bitcast.9), calls=%async_computation.4 | async-start | bytes 2555904 | tf_op jit(solution)/shard_map/all_to_all | solution.py:202
  80.0 0.0 copy-done.1
  80.0 2.9 %fusion.6 = (f32[320,512]{1,0:T(8,128)S(1)}, f32[320,512]{1,0:T(8,128)}) fusion(bf16[1,1664,512]{2,1,0:T(8,128)(2,1)S(1)} %copy-done.1, bf16[1,1,320,1664]{3,2,1,0:T(8,128)(2,1)} %param.9), kind=kOutput, calls=%fused_computation.9 | convolution fusion | flops 546570240 | bytes 4079616 | tf_op jit(solution)/shard_map/dot_general | solution.py:38
  83.0 4.4 %shard_map.87 = (bf16[320,1664]{1,0:T(8,128)(2,1)S(1)}, bf16[4,320,512]{2,1,0:T(8,128)(2,1)}, bf16[8,320,208]{2,1,0:T(8,128)(2,1)S(1)}) custom-call(s32[2]{0:T(128)S(1)} %pad_add_fusion.pos_ref, bf16[320,1664]{1,0:T(8,128)(2,1)S(1)} %bitcast.33, bf16[1664,512]{1,0:T(8,128)(2,1)} %bitcast.35, bf16[1664,512]{1,0:T(8,128)(2,1)} %bitcast.36, ...), custom_call_target="tpu_custom_call" | custom-call | tf_op jit(solution)/shard_map/pallas_call | solution.py:159
  87.4 1.5 copy.15
  88.9 0.0 copy-start.3
  88.9 21.7 %all-to-all-done.4 = bf16[4,320,416]{1,2,0:T(8,128)(2,1)} async-done(((bf16[4,320,416]{1,2,0:T(8,128)(2,1)}), bf16[4,320,416]{1,2,0:T(8,128)(2,1)}, u32[]{:S(2)}, u32[]{:S(2)}) %all-to-all-start.4) | async-done | bytes 1064992 | tf_op jit(solution)/shard_map/all_to_all | solution.py:202
  110.6 5.4 %all-to-all-start.1 = ((bf16[8,320,208]{1,2,0:T(8,128)(2,1)}), bf16[8,320,208]{1,2,0:T(8,128)(2,1)S(1)}, u32[]{:S(2)}, u32[]{:S(2)}) async-start(bf16[8,320,208]{1,2,0:T(8,128)(2,1)} %copy.15), calls=%async_computation.1 | async-start | bytes 2555904 | tf_op jit(solution)/shard_map/all_to_all | solution.py:218
  116.0 0.0 reduce-scatter.2.cloned.1.call-start
  116.0 0.0 copy-done.3
  116.0 2.3 %convolution_convert_fusion = bf16[1664,512]{1,0:T(8,128)(2,1)} fusion(bf16[320,1664]{1,0:T(8,128)(2,1)S(1)} %get-tuple-element.18, f32[320,512]{1,0:T(8,128)S(1)} %copy-done.3), kind=kOutput, calls=%fused_computation | convolution fusion | flops 546930688 | bytes 3424256 | tf_op jit(solution)/shard_map/dot_general | solution.py:38
  118.4 0.0 reduce-scatter.2.cloned.1.call-update
  118.4 13.8 %all-to-all-done.1 = bf16[8,320,208]{1,2,0:T(8,128)(2,1)S(1)} async-done(((bf16[8,320,208]{1,2,0:T(8,128)(2,1)}), bf16[8,320,208]{1,2,0:T(8,128)(2,1)S(1)}, u32[]{:S(2)}, u32[]{:S(2)}) %all-to-all-start.1) | async-done | bytes 1064992 | tf_op jit(solution)/shard_map/all_to_all | solution.py:218
  132.2 4.3 %all-to-all-start.3 = ((bf16[4,320,512]{2,1,0:T(8,128)(2,1)}), bf16[4,320,512]{2,1,0:T(8,128)(2,1)}, u32[]{:S(2)}, u32[]{:S(2)}) async-start(bf16[4,320,512]{2,1,0:T(8,128)(2,1)} %get-tuple-element.17), calls=%async_computation.3 | async-start | bytes 2621440 | tf_op jit(solution)/shard_map/all_to_all | solution.py:219
  136.5 0.7 copy.16.part_ref
  137.2 1.5 shard_map.88
  138.8 53.6 %all-to-all-done.3 = bf16[4,320,512]{2,1,0:T(8,128)(2,1)} async-done(((bf16[4,320,512]{2,1,0:T(8,128)(2,1)}), bf16[4,320,512]{2,1,0:T(8,128)(2,1)}, u32[]{:S(2)}, u32[]{:S(2)}) %all-to-all-start.3) | async-done | bytes 1310752 | tf_op jit(solution)/shard_map/all_to_all | solution.py:219
  192.4 8.8 %all-to-all-start.2 = ((bf16[32,24,128]{2,1,0:T(8,128)(2,1)}), bf16[32,24,128]{2,1,0:T(8,128)(2,1)S(1)}, u32[]{:S(2)}, u32[]{:S(2)}) async-start(bf16[32,24,128]{2,1,0:T(8,128)(2,1)} %bitcast.6), calls=%async_computation.2 | async-start | bytes 393216 | tf_op jit(solution)/shard_map/all_to_all | solution.py:224
  201.2 3.2 %fusion.1 = bf16[1,416,512]{2,1,0:T(8,128)(2,1)} fusion(bf16[4,320,416]{1,2,0:T(8,128)(2,1)} %all-to-all-done.4, bf16[4,320,512]{2,1,0:T(8,128)(2,1)} %all-to-all-done.3), kind=kOutput, calls=%fused_computation.3 | convolution fusion | flops 545472512 | bytes 2801664 | tf_op jit(solution)/shard_map/dot_general | solution.py:38
  204.4 15.4 %all-to-all-done.2 = bf16[32,24,128]{2,1,0:T(8,128)(2,1)S(1)} async-done(((bf16[32,24,128]{2,1,0:T(8,128)(2,1)}), bf16[32,24,128]{2,1,0:T(8,128)(2,1)S(1)}, u32[]{:S(2)}, u32[]{:S(2)}) %all-to-all-start.2) | async-done | bytes 196640 | tf_op jit(solution)/shard_map/all_to_all | solution.py:224
  219.8 0.4 shard_map.89
  220.2 0.7 copy.18
  220.9 0.0 reduce-scatter.2.cloned.1.call-done
Async XLA Ops:
  8.8 1.0 copy-start
  11.4 31.3 %collective-permute-start = (bf16[136,128]{1,0:T(8,128)(2,1)S(1)}, bf16[136,128]{1,0:T(8,128)(2,1)S(1)}, u32[]{:S(2)}, u32[]{:S(2)}) collective-permute-start(bf16[136,128]{1,0:T(8,128)(2,1)S(1)} %get-tuple-element.12), channel_id=1, source_target_pairs={{0,0},{4,28},{8,24},{12,20},{16,16},{20,12},{24,8},{28,4},{32,32},... | collective-permute-start | bytes 104456 | tf_op jit(solution)/shard_map/ppermute | solution.py:196
  19.9 22.9 %collective-permute-start.1 = (bf16[136,128]{1,0:T(8,128)(2,1)S(1)}, bf16[136,128]{1,0:T(8,128)(2,1)S(1)}, u32[]{:S(2)}, u32[]{:S(2)}) collective-permute-start(bf16[136,128]{1,0:T(8,128)(2,1)S(1)} %get-tuple-element.13), channel_id=1, source_target_pairs={{0,32},{4,60},{8,56},{12,52},{16,48},{20,44},{24,40},{28,36},{32,6... | collective-permute-start | bytes 104456 | tf_op jit(solution)/shard_map/ppermute | solution.py:196
  30.3 12.5 %collective-permute-start.2 = (bf16[136,128]{1,0:T(8,128)(2,1)S(1)}, bf16[136,128]{1,0:T(8,128)(2,1)S(1)}, u32[]{:S(2)}, u32[]{:S(2)}) collective-permute-start(bf16[136,128]{1,0:T(8,128)(2,1)S(1)} %get-tuple-element.14), channel_id=1, source_target_pairs={{0,64},{4,92},{8,88},{12,84},{16,80},{20,76},{24,72},{28,68},{32,9... | collective-permute-start | bytes 104456 | tf_op jit(solution)/shard_map/ppermute | solution.py:196
  39.4 12.2 %collective-permute-start.3 = (bf16[136,128]{1,0:T(8,128)(2,1)S(1)}, bf16[136,128]{1,0:T(8,128)(2,1)S(1)}, u32[]{:S(2)}, u32[]{:S(2)}) collective-permute-start(bf16[136,128]{1,0:T(8,128)(2,1)S(1)} %get-tuple-element.15), channel_id=1, source_target_pairs={{0,96},{4,124},{8,120},{12,116},{16,112},{20,108},{24,104},{28,100... | collective-permute-start | bytes 104456 | tf_op jit(solution)/shard_map/ppermute | solution.py:196
  53.0 6.0 %copy-start.2 = (bf16[1,1,320,1664]{3,2,1,0:T(8,128)(2,1)S(1)}, bf16[1,1,320,1664]{3,2,1,0:T(8,128)(2,1)}, u32[]{:S(2)}) copy-start(bf16[1,1,320,1664]{3,2,1,0:T(8,128)(2,1)} %param.9) | copy-start | bytes 3194884
  53.0 22.1 %all-to-all-start = ((bf16[8,40,1664]{2,1,0:T(8,128)(2,1)}), bf16[8,40,1664]{2,1,0:T(8,128)(2,1)S(1)}, u32[]{:S(2)}, u32[]{:S(2)}) async-start(bf16[8,40,1664]{2,1,0:T(8,128)(2,1)} %shard_map.86), calls=%async_computation | async-start | bytes 2129920 | tf_op jit(solution)/shard_map/all_to_all | solution.py:207
  75.0 5.0 %copy-start.1 = (bf16[1,1664,512]{2,1,0:T(8,128)(2,1)S(1)}, bf16[1,1664,512]{2,1,0:T(8,128)(2,1)}, u32[]{:S(2)}) copy-start(bf16[1,1664,512]{2,1,0:T(8,128)(2,1)} %param.10) | copy-start | bytes 5111812
  75.0 35.5 %all-to-all-start.4 = ((bf16[4,320,416]{1,2,0:T(8,128)(2,1)}), bf16[4,320,416]{1,2,0:T(8,128)(2,1)}, u32[]{:S(2)}, u32[]{:S(2)}) async-start(bf16[4,320,416]{1,2,0:T(8,128)(2,1)} %bitcast.9), calls=%async_computation.4 | async-start | bytes 2555904 | tf_op jit(solution)/shard_map/all_to_all | solution.py:202
  88.9 27.1 %copy-start.3 = (f32[320,512]{1,0:T(8,128)S(1)}, f32[320,512]{1,0:T(8,128)}, u32[]{:S(2)}) copy-start(f32[320,512]{1,0:T(8,128)} %get-tuple-element.26) | copy-start | bytes 1966084
  110.6 21.6 %all-to-all-start.1 = ((bf16[8,320,208]{1,2,0:T(8,128)(2,1)}), bf16[8,320,208]{1,2,0:T(8,128)(2,1)S(1)}, u32[]{:S(2)}, u32[]{:S(2)}) async-start(bf16[8,320,208]{1,2,0:T(8,128)(2,1)} %copy.15), calls=%async_computation.1 | async-start | bytes 2555904 | tf_op jit(solution)/shard_map/all_to_all | solution.py:218
  116.0 104.9 %reduce-scatter.2.cloned.1.call-start = ((), (), s32[]{:S(2)}) async-start(), calls=%async_computation.6 | async-start | bytes 2129920 | tf_op jit(solution)/shard_map/reduce_scatter | solution.py:221
  132.2 60.2 %all-to-all-start.3 = ((bf16[4,320,512]{2,1,0:T(8,128)(2,1)}), bf16[4,320,512]{2,1,0:T(8,128)(2,1)}, u32[]{:S(2)}, u32[]{:S(2)}) async-start(bf16[4,320,512]{2,1,0:T(8,128)(2,1)} %get-tuple-element.17), calls=%async_computation.3 | async-start | bytes 2621440 | tf_op jit(solution)/shard_map/all_to_all | solution.py:219
  192.4 27.4 %all-to-all-start.2 = ((bf16[32,24,128]{2,1,0:T(8,128)(2,1)}), bf16[32,24,128]{2,1,0:T(8,128)(2,1)S(1)}, u32[]{:S(2)}, u32[]{:S(2)}) async-start(bf16[32,24,128]{2,1,0:T(8,128)(2,1)} %bitcast.6), calls=%async_computation.2 | async-start | bytes 393216 | tf_op jit(solution)/shard_map/all_to_all | solution.py:224
Sparse Core Ops, SparseCore 0:
  120.8 65.3 reduce-scatter.1

commit v2 on v1

--- a/solution.py
+++ b/solution.py
@@ -19,10 +19,14 @@
 SENDS = EXP // REP
 PACKED = 136
 BACK = 24
+HALF = LANES // 2
+PART = 528
 SHARE = SENDS * CAP
+ORDER = (2, 1, 3, 0)
 
 VMEM = pl.BlockSpec(memory_space=pltpu.VMEM)
 SMEM = pl.BlockSpec(memory_space=pltpu.SMEM)
+HBM = pl.BlockSpec(memory_space=pltpu.HBM)
 PARAMS = pltpu.CompilerParams(vmem_limit_bytes=48 * 1024 * 1024)
 
 
@@ -36,14 +40,23 @@
 
 def dot(a, b, dims=((1,), (0,))):
     return lax.dot_general(a, b, (dims, ((), ())), preferred_element_type=jnp.float32)
+
+
+def in_order(k):
+    step = jnp.full_like(k, ORDER[0])
+    for q in range(1, SENDS):
+        step = jnp.where(k == q, ORDER[q], step)
+    return step
 
 
 def dispatch_kernel(pos_ref, ids_ref, gates_ref, grad_ref, o0, o1, o2, o3, code_ref):
     rep, src = pos_ref[0], pos_ref[1]
     lane = iota((TOK, LANES), 1)
     before = hot(iota((TOK, TOK), 0) > iota((TOK, TOK), 1))
-    first = ids_ref[:, 0:1]
-    second = ids_ref[:, 1:2]
+    ids = jnp.concatenate([ids_ref[...], jnp.zeros((6, TOK), jnp.int32)], axis=0).T
+    gates = jnp.concatenate([gates_ref[...], jnp.zeros((6, TOK), jnp.float32)], axis=0).T
+    first = ids[:, 0:1]
+    second = ids[:, 1:2]
     hot0 = hot(first == lane)
     hot1 = hot(second == lane)
     count0 = jnp.sum(hot0.astype(jnp.float32), axis=0, keepdims=True)
@@ -60,11 +73,11 @@
     col = iota((1, LANES), 1)
     k = col >> 4
     c = col & 15
-    expert = ((rep - src) & 7) + 8 * (((src >> 3) + k) & 3)
+    expert = ((rep - src) & 7) + 8 * (((src >> 3) + in_order(k)) & 3)
     wanted = jnp.where((c < CAP) & (k < SENDS), expert * 16 + c, -2)
     grad = grad_ref[...].astype(jnp.float32)
-    scaled0 = (gates_ref[:, 0:1] * grad).astype(jnp.bfloat16)
-    scaled1 = (gates_ref[:, 1:2] * grad).astype(jnp.bfloat16)
+    scaled0 = (gates[:, 0:1] * grad).astype(jnp.bfloat16)
+    scaled1 = (gates[:, 1:2] * grad).astype(jnp.bfloat16)
     rows = dot(hot(target0 == wanted), scaled0, ((0,), (0,))) + dot(
         hot(target1 == wanted), scaled1, ((0,), (0,))
     )
@@ -109,38 +122,75 @@
         out_ref[q] = share
 
 
-def middle_kernel(pos_ref, got_ref, w_in_ref, w_out_ref, slope_ref, up_ref, dhid_ref, part_ref):
-    exp = pos_ref[1]
+def fold(rows):
+    half = rows.shape[0] // 2
+    return jnp.concatenate([rows[:half], rows[half:]], axis=1)
+
+
+def unfold(rows):
+    return jnp.concatenate([rows[:, :HALF], rows[:, HALF:]], axis=0)
+
+
+def landing(exp):
     j = iota((1, SLOTS), 1)
     block = lax.div(j, SHARE)
     rest = j - block * SHARE
     k = lax.div(rest, CAP)
-    source = ((block - exp) & 7) + 8 * (((exp >> 3) - k) & 3)
-    place = source * CAP + (rest - k * CAP)
-    up = dot(hot(iota((SLOTS, SLOTS), 0) == place), got_ref[...]).astype(jnp.bfloat16)
-    up_ref[...] = up
+    source = ((block - exp) & 7) + 8 * (((exp >> 3) - in_order(k)) & 3)
+    return hot(iota((SLOTS, SLOTS), 0) == source * CAP + (rest - k * CAP))
+
+
+def hidden_kernel(inputs_ref, w_in_ref, act_ref, slope_ref, wide_ref):
+    inputs = inputs_ref[...]
+    hidden = dot(inputs, w_in_ref[...])
+    cdf = 0.5 * (1.0 + lax.erf(hidden * SQRT_HALF))
+    act_ref[...] = (hidden * cdf).astype(jnp.bfloat16)
+    slope_ref[...] = cdf + hidden * INV_ROOT_TAU * jnp.exp(-0.5 * hidden * hidden)
+    wide_ref[...] = inputs.T
+
+
+def middle_kernel(
+    pos_ref, got_ref, wide_ref, act_ref, w_out_ref, w_in_ref, slope_ref,
+    part_ref, terms_hbm, terms_ref, sems,
+):
+    up = dot(landing(pos_ref[1]), got_ref[...]).astype(jnp.bfloat16)
     dhid = (dot(up, w_out_ref[...]) * slope_ref[...]).astype(jnp.bfloat16)
+    copies = []
     for q in range(NODE):
-        dhid_ref[q] = dhid
+        rows = slice(ROWS * q, ROWS * (q + 1))
+        terms_ref[q, :ROWS] = dot(wide_ref[rows, :], dhid).astype(jnp.bfloat16)
+    term = dot(up, act_ref[...], ((0,), (0,)))
+    for q in range(NODE):
+        terms_ref[q, ROWS:] = term[ROWS * q : ROWS * (q + 1)].astype(jnp.bfloat16)
+        copies.append(pltpu.make_async_copy(terms_ref.at[q], terms_hbm.at[q], sems.at[q]))
+        copies[-1].start()
     for q in range(REP):
-        part_ref[q] = dot(dhid, w_in_ref[COLS * q : COLS * (q + 1), :], ((1,), (1,))).astype(
-            jnp.bfloat16
-        )
+        block = dot(w_in_ref[COLS * q : COLS * (q + 1), :], dhid, ((1,), (1,)))
+        part_ref[q, 0:COLS] = block[:, :LANES].astype(jnp.bfloat16)
+        part_ref[q, COLS : 2 * COLS] = block[:, LANES : 2 * LANES].astype(jnp.bfloat16)
+        last = fold(block[:, 2 * LANES :])
+        last = jnp.concatenate([last, jnp.zeros((8, LANES), jnp.float32)], axis=0)
+        part_ref[q, 2 * COLS :] = last.astype(jnp.bfloat16)
+    for copy in copies:
+        copy.wait()
 
 
 def back_kernel(part_ref, out_ref):
     total = part_ref[0].astype(jnp.float32)
     for q in range(1, REP):
         total = total + part_ref[q].astype(jnp.float32)
+    last = unfold(total[2 * COLS : 2 * COLS + COLS // 2])
+    total = jnp.concatenate([total[:COLS], total[COLS : 2 * COLS]], axis=1)
+    total = jnp.concatenate([total, last], axis=1)
+    total = jnp.concatenate([total, jnp.zeros((2 * LANES - COLS, SLOTS), jnp.float32)], axis=0)
     total = total.astype(jnp.bfloat16)
-    tail = dot(total, hot(iota((COLS, LANES), 0) == iota((COLS, LANES), 1) + LANES))
     m = iota((EXP * BACK, SLOTS), 0)
     s = lax.div(m, BACK)
     q = m - s * BACK
     j = iota((EXP * BACK, SLOTS), 1)
     one = hot((j == s * CAP + q) & (q < CAP))
     two = hot((j == s * CAP + q - CAP) & (q >= CAP) & (q < 2 * CAP))
-    out = dot(one, total[:, :LANES]) + dot(two, tail.astype(jnp.bfloat16))
+    out = dot(one, total[:LANES], ((1,), (1,))) + dot(two, total[LANES:], ((1,), (1,)))
     out_ref[...] = out.astype(jnp.bfloat16)
 
 
@@ -149,18 +199,19 @@
     code0 = code_ref[:, 0:1]
     code1 = code_ref[:, 1:2]
     back = back_ref[...]
-    head = dot(hot((lane == code0) | (lane == code1)), back)
-    tail = dot(hot((lane == code0 + CAP) | (lane == code1 + CAP)), back)
-    out_ref[:, :LANES] = head.astype(jnp.bfloat16)
-    out_ref[:, LANES:] = tail[:, : COLS - LANES].astype(jnp.bfloat16)
-
-
-def call(kernel, out, in_specs, *args):
+    head = dot(back, hot((lane == code0) | (lane == code1)), ((0,), (1,)))
+    tail = dot(back, hot((lane == code0 + CAP) | (lane == code1 + CAP)), ((0,), (1,)))
+    out_ref[:LANES] = head.astype(jnp.bfloat16)
+    out_ref[LANES:] = tail[: COLS - LANES].astype(jnp.bfloat16)
+
+
+def call(kernel, out, in_specs, *args, scratch=(), out_specs=None):
     return pl.pallas_call(
         kernel,
         out_shape=out,
         in_specs=in_specs,
-        out_specs=jax.tree.map(lambda _: VMEM, out),
+        out_specs=out_specs or jax.tree.map(lambda _: VMEM, out),
+        scratch_shapes=list(scratch),
         compiler_params=PARAMS,
     )(*args)
 
@@ -179,7 +230,8 @@
 
 
 def local(grad_out, gates, expert_ids, saved_inputs, w_in, w_out):
-    pos = jnp.stack([lax.axis_index("rep"), lax.axis_index("exp")]).astype(jnp.int32)
+    pos = jnp.stack([lax.axis_index("rep"), lax.axis_index("exp"), lax.axis_index("node")])
+    pos = pos.astype(jnp.int32)
     inputs = saved_inputs[0, 0]
     proj_in = w_in[0]
     proj_out = w_out[0]
@@ -189,46 +241,51 @@
         [shape(PACKED, LANES)] * SENDS + [shape(TOK, 2, dtype=jnp.int32)],
         [SMEM] + [VMEM] * 3,
         pos,
-        expert_ids,
-        gates,
+        expert_ids.T,
+        gates.T,
         grad_out,
     )
-    landed = [lax.ppermute(p, ("rep", "exp"), send_pairs(k)) for k, p in enumerate(packed)]
-
-    hidden = dot(inputs, proj_in)
-    cdf = 0.5 * (1.0 + lax.erf(hidden * SQRT_HALF))
-    act = (hidden * cdf).astype(jnp.bfloat16)
-    slope = cdf + hidden * INV_ROOT_TAU * jnp.exp(-0.5 * hidden * hidden)
-    input_cols = lax.all_to_all(
-        inputs.reshape(SLOTS, NODE, ROWS).transpose(1, 0, 2), "node", 0, 0, tiled=True
-    )
-
+    landed = [lax.ppermute(p, ("rep", "exp"), send_pairs(k)) for k, p in zip(ORDER, packed)]
+
+    act, slope, wide = call(
+        hidden_kernel,
+        [shape(SLOTS, HID), shape(SLOTS, HID, dtype=jnp.float32), shape(WIDTH, SLOTS)],
+        [VMEM] * 2,
+        inputs,
+        proj_in,
+    )
+
+    *landed, slope, wide, act = lax.optimization_barrier((*landed, slope, wide, act))
     shares = call(unpack_kernel, shape(REP, SHARE, WIDTH), [VMEM] * SENDS, *landed)
     got = lax.all_to_all(shares, "rep", 0, 0, tiled=True).reshape(SLOTS, WIDTH)
-    up, dhid, part = call(
+    part, terms = call(
         middle_kernel,
-        [shape(SLOTS, WIDTH), shape(NODE, SLOTS, HID), shape(REP, SLOTS, COLS)],
-        [SMEM] + [VMEM] * 4,
+        [shape(REP, PART, LANES), shape(NODE, 2 * ROWS, HID)],
+        [SMEM] + [VMEM] * 6,
         pos,
         got,
+        wide,
+        act,
+        proj_out,
         proj_in,
-        proj_out,
         slope,
+        scratch=[
+            pltpu.VMEM((NODE, 2 * ROWS, HID), jnp.bfloat16),
+            pltpu.SemaphoreType.DMA((NODE,)),
+        ],
+        out_specs=[VMEM, HBM],
+    )
+    summed = lax.psum_scatter(
+        terms.reshape(NODE * 2 * ROWS, HID), "node", scatter_dimension=0, tiled=True
     )
     part = lax.all_to_all(part, "rep", 0, 0, tiled=True)
-    dhid_all = lax.all_to_all(dhid, "node", 0, 0, tiled=True)
-    grad_b = dot(up, act, ((0,), (0,))).astype(jnp.bfloat16)
-    grad_w_out = lax.psum_scatter(grad_b, "node", scatter_dimension=0, tiled=True)
 
     back = call(back_kernel, shape(EXP * BACK, LANES), [VMEM], part)
     back = lax.all_to_all(back.reshape(EXP, BACK, LANES), "exp", 0, 0, tiled=True)
     grad_inputs = call(
-        combine_kernel, shape(TOK, COLS), [VMEM] * 2, code, back.reshape(EXP * BACK, LANES)
-    )
-    grad_w_in = dot(
-        input_cols.reshape(NODE * SLOTS, ROWS), dhid_all.reshape(NODE * SLOTS, HID), ((0,), (0,))
-    ).astype(jnp.bfloat16)
-    return grad_inputs, grad_w_in[None], grad_w_out[None]
+        combine_kernel, shape(COLS, TOK), [VMEM] * 2, code, back.reshape(EXP * BACK, LANES)
+    )
+    return grad_inputs.T, summed[None, :ROWS], summed[None, ROWS:]
 
 
 def solution(mesh):

time: 228 us -> 163 us (0.71)
  waiting for transfers between devices: 128 us -> 20.2 us
  blocking collectives: 0 us -> 75.6 us
  starting transfers between devices: 60.8 us -> 34 us
  matrix products: 8.42 us -> 0 us
    all_to_all x5 -> x0, waiting for transfers between devices: 119 us -> none  [the longest x1 53.6 us: local(): dhid_all = lax.all_to_all(dhid, 'node', 0, 0, tiled=True)]
    all_to_all x0 -> x3, blocking collectives: none -> 75.6 us  [the longest x1 37.1 us: local(): lax.all_to_all(back.reshape(EXP, BACK, LANES), 'exp', 0, 0, tiled=True)]
    all_to_all x5 -> x0, starting transfers between devices: 29.5 us -> none  [the longest x1 8.77 us: local(): lax.all_to_all(back.reshape(EXP, BACK, LANES), 'exp', 0, 0, tiled=True)]
    reduce_scatter x1, waiting for transfers between devices: 0.01 us -> 20.1 us  [local(): lax.psum_scatter(terms.reshape(NODE * 2 * ROWS, HID), 'node', scatter_dim...]
    ppermute x4, waiting for transfers between devices: 8.8 us -> 0.01 us  [local(): lax.ppermute(p, ('rep', 'exp'), send_pairs(k))]
    dot_general x3 -> x0, matrix products: 8.42 us -> none  [dot(): lax.dot_general(a, b, (dims, ((), ())), preferred_element_type=jnp.float32)]
    ppermute x4, starting transfers between devices: 31.3 us -> 34 us  [local(): lax.ppermute(p, ('rep', 'exp'), send_pairs(k))]
    pallas_call x5 -> x6, Pallas kernels: 9.26 us -> 11.1 us  [call(): pl.pallas_call(kernel, out_shape=out, in_specs=in_specs, out_specs=out_sp...]
  transfers between devices with their start and end apart: 10 -> 5, of which waited for: 6 -> 1; matrix products, arithmetic and copies ran while one was open for 6% -> 0% of each run, Pallas kernels for 3% -> 2%
where the time goes in v2:
time: 163 us; the launch traced here: 162 us
  blocking collectives  75.6 us (46%)
  starting transfers between devices  34 us (21%)
  waiting for transfers between devices  20.2 us (12%)
  between operations  14.2 us (9%)
  Pallas kernels  11.1 us (7%)
  local copies, waits for them, and re-layouts  7.14 us (4%)
    all_to_all x1, blocking collectives, local(): lax.all_to_all(back.reshape(EXP, BACK, LANES), 'exp', 0, 0, tiled=True)  37.1 us
    ppermute x4, starting transfers between devices, local(): lax.ppermute(p, ('rep', 'exp'), send_pairs(k))  34 us
    all_to_all x1, blocking collectives, local(): got = lax.all_to_all(shares, 'rep', 0, 0, tiled=True).reshape(SLOTS, WIDTH)  21.4 us
    reduce_scatter x1, waiting for transfers between devices, local(): lax.psum_scatter(terms.reshape(NODE * 2 * ROWS, HID), 'node', scatter_dim...  20.1 us
    all_to_all x1, blocking collectives, local(): part = lax.all_to_all(part, 'rep', 0, 0, tiled=True)  17.1 us
    pallas_call x6, Pallas kernels, call(): pl.pallas_call(kernel, out_shape=out, in_specs=in_specs, out_specs=out_sp...  11.1 us
    unnamed x12, local copies, waits for them, and re-layouts  5.05 us
  transfers between devices with their start and end apart: 5, of which 1 were waited for; matrix products, arithmetic and copies ran while one was open for 0% of the time, Pallas kernels for 2%

profile of v2, /device:TPU:1, one launch (start us, length us, event | category | flops | bytes accessed | tf_op | source)
XLA Modules:
  0.0 162.3 jit_solution(8225440723005615248)
XLA Ops:
  7.2 0.0 reduce-scatter.2.cloned.1.call-start
  7.2 0.1 pad_add_fusion.pos_ref
  7.3 0.0 copy-start.3
  7.3 1.0 copy-done.3
  8.3 0.0 copy-start.4
  8.3 0.7 copy-done.4
  9.0 0.0 copy-start.5
  9.0 0.7 copy-done.5
  9.7 1.8 %shard_map.85 = (bf16[136,128]{1,0:T(8,128)(2,1)S(1)}, bf16[136,128]{1,0:T(8,128)(2,1)S(1)}, bf16[136,128]{1,0:T(8,128)(2,1)S(1)}, bf16[136,128]{1,0:T(8,128)(2,1)S(1)}, s32[128,2]{1,0:T(8,128)S(1)}) custom-call(s32[3]{0:T(128)S(1)} %pad_add_fusion.pos_ref, s32[2,128]{1,0:T(2,128)S(1)} %bitcast.24, f32[2,128]{1,0:T(2,128)S(1)} %bitcast.25, ...), custom_call_target="tpu_custom_call" | custom-call | tf_op jit(solution)/shard_map/pallas_call | solution.py:209
  11.4 19.9 %collective-permute-start = (bf16[136,128]{1,0:T(8,128)(2,1)S(1)}, bf16[136,128]{1,0:T(8,128)(2,1)S(1)}, u32[]{:S(2)}, u32[]{:S(2)}) collective-permute-start(bf16[136,128]{1,0:T(8,128)(2,1)S(1)} %get-tuple-element.21), channel_id=1, source_target_pairs={{0,64},{4,92},{8,88},{12,84},{16,80},{20,76},{24,72},{28,68},{32,9... | collective-permute-start | bytes 104456 | tf_op jit(solution)/shard_map/ppermute | solution.py:248
  31.4 5.8 %collective-permute-start.1 = (bf16[136,128]{1,0:T(8,128)(2,1)S(1)}, bf16[136,128]{1,0:T(8,128)(2,1)S(1)}, u32[]{:S(2)}, u32[]{:S(2)}) collective-permute-start(bf16[136,128]{1,0:T(8,128)(2,1)S(1)} %get-tuple-element.22), channel_id=1, source_target_pairs={{0,32},{4,60},{8,56},{12,52},{16,48},{20,44},{24,40},{28,36},{32,6... | collective-permute-start | bytes 104456 | tf_op jit(solution)/shard_map/ppermute | solution.py:248
  37.2 1.9 %collective-permute-start.2 = (bf16[136,128]{1,0:T(8,128)(2,1)S(1)}, bf16[136,128]{1,0:T(8,128)(2,1)S(1)}, u32[]{:S(2)}, u32[]{:S(2)}) collective-permute-start(bf16[136,128]{1,0:T(8,128)(2,1)S(1)} %get-tuple-element.23), channel_id=1, source_target_pairs={{0,96},{4,124},{8,120},{12,116},{16,112},{20,108},{24,104},{28,100... | collective-permute-start | bytes 104456 | tf_op jit(solution)/shard_map/ppermute | solution.py:248
  39.1 6.3 %collective-permute-start.3 = (bf16[136,128]{1,0:T(8,128)(2,1)S(1)}, bf16[136,128]{1,0:T(8,128)(2,1)S(1)}, u32[]{:S(2)}, u32[]{:S(2)}) collective-permute-start(bf16[136,128]{1,0:T(8,128)(2,1)S(1)} %get-tuple-element.24), channel_id=1, source_target_pairs={{0,0},{4,28},{8,24},{12,20},{16,16},{20,12},{24,8},{28,4},{32,32},... | collective-permute-start | bytes 104456 | tf_op jit(solution)/shard_map/ppermute | solution.py:248
  45.5 0.0 copy-start
  45.5 1.4 copy-done
  46.9 0.0 copy-start.2
  46.9 1.2 copy-done.2
  48.2 1.0 shard_map.86
  49.1 0.0 collective-permute-done.i0
  49.1 0.0 collective-permute-done.1.i1
  49.2 0.0 collective-permute-done.2.i2
  49.2 0.0 collective-permute-done.3.i3
  49.2 0.4 shard_map.87
  49.5 0.0 copy-start.1
  49.6 21.4 %all_to_all.15 = bf16[8,40,1664]{2,1,0:T(8,128)(2,1)S(1)} all-to-all(bf16[8,40,1664]{2,1,0:T(8,128)(2,1)S(1)} %shard_map.87), channel_id=1, replica_groups=mesh['rep'=8,'exp'=32,'node'=4] {'rep'}, dimensions={0} | all-to-all | bytes 2129920 | tf_op jit(solution)/shard_map/all_to_all | solution.py:260
  70.9 0.0 copy-done.1
  70.9 6.1 %shard_map.88 = (bf16[8,528,128]{2,1,0:T(8,128)(2,1)S(1)}, bf16[4,832,512]{2,1,0:T(8,128)(2,1)}) custom-call(s32[3]{0:T(128)S(1)} %pad_add_fusion.pos_ref, bf16[320,1664]{1,0:T(8,128)(2,1)S(1)} %bitcast.19, bf16[1664,320]{1,0:T(8,128)(2,1)S(1)} %get-tuple-element.32.wide_ref, bf16[320,512]{1,0:T(8,128)(2,1)S(1)} %get-tuple-element.33.act_ref, ...), custom_call_target="tpu_custom_call" | custom-call | tf_op jit(solution)/shard_map/pallas_call | solution.py:209
  77.1 0.0 reduce-scatter.2.cloned.1.call-update
  77.1 17.1 %all_to_all.16.part_ref = bf16[8,528,128]{2,1,0:T(8,128)(2,1)S(1)} all-to-all(bf16[8,528,128]{2,1,0:T(8,128)(2,1)S(1)} %get-tuple-element.35), channel_id=1, replica_groups=mesh['rep'=8,'exp'=32,'node'=4] {'rep'}, dimensions={0} | all-to-all | bytes 2162688 | tf_op jit(solution)/shard_map/all_to_all | solution.py:281
  94.2 0.8 shard_map.89
  95.0 37.1 %all_to_all.17 = bf16[32,24,128]{2,1,0:T(8,128)(2,1)S(1)} all-to-all(bf16[32,24,128]{2,1,0:T(8,128)(2,1)S(1)} %bitcast.22), channel_id=1, replica_groups=mesh['rep'=8,'exp'=32,'node'=4] {'exp'}, dimensions={0} | all-to-all | bytes 393216 | tf_op jit(solution)/shard_map/all_to_all | solution.py:284
  132.1 1.1 shard_map.90
  133.2 20.1 %reduce-scatter.2.cloned.1.call-done = bf16[832,512]{1,0:T(8,128)(2,1)} async-done(((bf16[3328,512]{1,0:T(8,128)(2,1)}), bf16[832,512]{1,0:T(8,128)(2,1)}) %reduce-scatter.2.cloned.1.call-update) | async-done | bytes 851984 | tf_op jit(solution)/shard_map/reduce_scatter | solution.py:278
  153.3 2.1 %slice_bitcast_fusion = (bf16[1,416,512]{2,1,0:T(8,128)(2,1)}, bf16[1,416,512]{2,1,0:T(8,128)(2,1)}) fusion(bf16[832,512]{1,0:T(8,128)(2,1)} %reduce-scatter.2.cloned.1.call-done), kind=kLoop, calls=%fused_computation | loop fusion | bytes 1703936 | tf_op jit(solution)/shard_map/broadcast_in_dim | solution.py:288
Async XLA Ops:
  7.2 146.2 %reduce-scatter.2.cloned.1.call-start = ((), (), s32[]{:S(2)}) async-start(), calls=%async_computation.4 | async-start | bytes 4259840 | tf_op jit(solution)/shard_map/reduce_scatter | solution.py:278
  7.3 1.0 copy-start.3
  8.3 0.7 copy-start.4
  9.0 0.7 copy-start.5
  11.4 37.7 %collective-permute-start = (bf16[136,128]{1,0:T(8,128)(2,1)S(1)}, bf16[136,128]{1,0:T(8,128)(2,1)S(1)}, u32[]{:S(2)}, u32[]{:S(2)}) collective-permute-start(bf16[136,128]{1,0:T(8,128)(2,1)S(1)} %get-tuple-element.21), channel_id=1, source_target_pairs={{0,64},{4,92},{8,88},{12,84},{16,80},{20,76},{24,72},{28,68},{32,9... | collective-permute-start | bytes 104456 | tf_op jit(solution)/shard_map/ppermute | solution.py:248
  31.4 17.8 %collective-permute-start.1 = (bf16[136,128]{1,0:T(8,128)(2,1)S(1)}, bf16[136,128]{1,0:T(8,128)(2,1)S(1)}, u32[]{:S(2)}, u32[]{:S(2)}) collective-permute-start(bf16[136,128]{1,0:T(8,128)(2,1)S(1)} %get-tuple-element.22), channel_id=1, source_target_pairs={{0,32},{4,60},{8,56},{12,52},{16,48},{20,44},{24,40},{28,36},{32,6... | collective-permute-start | bytes 104456 | tf_op jit(solution)/shard_map/ppermute | solution.py:248
  37.2 12.0 %collective-permute-start.2 = (bf16[136,128]{1,0:T(8,128)(2,1)S(1)}, bf16[136,128]{1,0:T(8,128)(2,1)S(1)}, u32[]{:S(2)}, u32[]{:S(2)}) collective-permute-start(bf16[136,128]{1,0:T(8,128)(2,1)S(1)} %get-tuple-element.23), channel_id=1, source_target_pairs={{0,96},{4,124},{8,120},{12,116},{16,112},{20,108},{24,104},{28,100... | collective-permute-start | bytes 104456 | tf_op jit(solution)/shard_map/ppermute | solution.py:248
  39.1 10.0 %collective-permute-start.3 = (bf16[136,128]{1,0:T(8,128)(2,1)S(1)}, bf16[136,128]{1,0:T(8,128)(2,1)S(1)}, u32[]{:S(2)}, u32[]{:S(2)}) collective-permute-start(bf16[136,128]{1,0:T(8,128)(2,1)S(1)} %get-tuple-element.24), channel_id=1, source_target_pairs={{0,0},{4,28},{8,24},{12,20},{16,16},{20,12},{24,8},{28,4},{32,32},... | collective-permute-start | bytes 104456 | tf_op jit(solution)/shard_map/ppermute | solution.py:248
  45.5 1.5 copy-start
  46.9 1.2 copy-start.2
  49.5 21.4 %copy-start.1 = (bf16[1,1664,512]{2,1,0:T(8,128)(2,1)S(1)}, bf16[1,1664,512]{2,1,0:T(8,128)(2,1)}, u32[]{:S(2)}) copy-start(bf16[1,1664,512]{2,1,0:T(8,128)(2,1)} %param.11) | copy-start | bytes 5111812
Sparse Core Ops, SparseCore 0:
  77.2 76.1 reduce-scatter.1

commit v3 on v2

--- a/solution.py
+++ b/solution.py
@@ -9,6 +9,9 @@
 INV_ROOT_TAU = 0.3989422804014327
 
 REP, EXP, NODE = 8, 32, 4
+X, PAIR = 4, 2
+ALONG_X = [[PAIR * x + y for x in range(X)] for y in range(PAIR)]
+NEIGHBOUR = [(r, r ^ 1) for r in range(REP)]
 TOK, WIDTH, CAP = 128, 1664, 10
 SLOTS = EXP * CAP
 HID = 512
@@ -131,17 +134,18 @@
     return jnp.concatenate([rows[:, :HALF], rows[:, HALF:]], axis=0)
 
 
-def landing(exp):
+def places(exp):
     j = iota((1, SLOTS), 1)
     block = lax.div(j, SHARE)
     rest = j - block * SHARE
     k = lax.div(rest, CAP)
     source = ((block - exp) & 7) + 8 * (((exp >> 3) - in_order(k)) & 3)
-    return hot(iota((SLOTS, SLOTS), 0) == source * CAP + (rest - k * CAP))
-
-
-def hidden_kernel(inputs_ref, w_in_ref, act_ref, slope_ref, wide_ref):
-    inputs = inputs_ref[...]
+    return source * CAP + (rest - k * CAP)
+
+
+def hidden_kernel(pos_ref, inputs_ref, w_in_ref, act_ref, slope_ref, wide_ref):
+    order = hot(iota((SLOTS, SLOTS), 0) == places(pos_ref[1]))
+    inputs = dot(order, inputs_ref[...], ((0,), (0,))).astype(jnp.bfloat16)
     hidden = dot(inputs, w_in_ref[...])
     cdf = 0.5 * (1.0 + lax.erf(hidden * SQRT_HALF))
     act_ref[...] = (hidden * cdf).astype(jnp.bfloat16)
@@ -150,35 +154,59 @@
 
 
 def middle_kernel(
-    pos_ref, got_ref, wide_ref, act_ref, w_out_ref, w_in_ref, slope_ref,
-    part_ref, terms_hbm, terms_ref, sems,
+    got_ref, wide_ref, act_ref, w_out_ref, slope_ref, dhid_ref, terms_hbm, terms_ref, sems
 ):
-    up = dot(landing(pos_ref[1]), got_ref[...]).astype(jnp.bfloat16)
+    up = got_ref[...]
     dhid = (dot(up, w_out_ref[...]) * slope_ref[...]).astype(jnp.bfloat16)
+    dhid_ref[...] = dhid
+    term = dot(up, act_ref[...], ((0,), (0,)))
     copies = []
     for q in range(NODE):
         rows = slice(ROWS * q, ROWS * (q + 1))
+        terms_ref[q, ROWS:] = term[rows].astype(jnp.bfloat16)
         terms_ref[q, :ROWS] = dot(wide_ref[rows, :], dhid).astype(jnp.bfloat16)
-    term = dot(up, act_ref[...], ((0,), (0,)))
-    for q in range(NODE):
-        terms_ref[q, ROWS:] = term[ROWS * q : ROWS * (q + 1)].astype(jnp.bfloat16)
         copies.append(pltpu.make_async_copy(terms_ref.at[q], terms_hbm.at[q], sems.at[q]))
         copies[-1].start()
+    for copy in copies:
+        copy.wait()
+
+
+def split_kernel(summed_hbm, in_hbm, out_hbm, sems):
+    copies = [
+        pltpu.make_async_copy(summed_hbm.at[:ROWS], in_hbm, sems.at[0]),
+        pltpu.make_async_copy(summed_hbm.at[ROWS:], out_hbm, sems.at[1]),
+    ]
+    for copy in copies:
+        copy.start()
+    for copy in copies:
+        copy.wait()
+
+
+def part_kernel(dhid_ref, w_in_ref, part_ref):
+    dhid = dhid_ref[...]
     for q in range(REP):
         block = dot(w_in_ref[COLS * q : COLS * (q + 1), :], dhid, ((1,), (1,)))
-        part_ref[q, 0:COLS] = block[:, :LANES].astype(jnp.bfloat16)
-        part_ref[q, COLS : 2 * COLS] = block[:, LANES : 2 * LANES].astype(jnp.bfloat16)
+        x, y = divmod(q, PAIR)
+        part_ref[x, y, 0:COLS] = block[:, :LANES].astype(jnp.bfloat16)
+        part_ref[x, y, COLS : 2 * COLS] = block[:, LANES : 2 * LANES].astype(jnp.bfloat16)
         last = fold(block[:, 2 * LANES :])
         last = jnp.concatenate([last, jnp.zeros((8, LANES), jnp.float32)], axis=0)
-        part_ref[q, 2 * COLS :] = last.astype(jnp.bfloat16)
-    for copy in copies:
-        copy.wait()
-
-
-def back_kernel(part_ref, out_ref):
-    total = part_ref[0].astype(jnp.float32)
-    for q in range(1, REP):
-        total = total + part_ref[q].astype(jnp.float32)
+        part_ref[x, y, 2 * COLS :] = last.astype(jnp.bfloat16)
+
+
+def sum_kernel(pos_ref, part_ref, keep_ref, send_ref):
+    mine = pos_ref[0] & 1
+    keep = part_ref[0, mine].astype(jnp.float32)
+    send = part_ref[0, 1 - mine].astype(jnp.float32)
+    for q in range(1, X):
+        keep = keep + part_ref[q, mine].astype(jnp.float32)
+        send = send + part_ref[q, 1 - mine].astype(jnp.float32)
+    keep_ref[...] = keep
+    send_ref[...] = send.astype(jnp.bfloat16)
+
+
+def back_kernel(pos_ref, keep_ref, other_ref, out_ref):
+    total = keep_ref[...] + other_ref[...].astype(jnp.float32)
     last = unfold(total[2 * COLS : 2 * COLS + COLS // 2])
     total = jnp.concatenate([total[:COLS], total[COLS : 2 * COLS]], axis=1)
     total = jnp.concatenate([total, last], axis=1)
@@ -187,9 +215,9 @@
     m = iota((EXP * BACK, SLOTS), 0)
     s = lax.div(m, BACK)
     q = m - s * BACK
-    j = iota((EXP * BACK, SLOTS), 1)
-    one = hot((j == s * CAP + q) & (q < CAP))
-    two = hot((j == s * CAP + q - CAP) & (q >= CAP) & (q < 2 * CAP))
+    place = places(pos_ref[1])
+    one = hot((place == s * CAP + q) & (q < CAP))
+    two = hot((place == s * CAP + q - CAP) & (q >= CAP) & (q < 2 * CAP))
     out = dot(one, total[:LANES], ((1,), (1,))) + dot(two, total[LANES:], ((1,), (1,)))
     out_ref[...] = out.astype(jnp.bfloat16)
 
@@ -250,7 +278,8 @@
     act, slope, wide = call(
         hidden_kernel,
         [shape(SLOTS, HID), shape(SLOTS, HID, dtype=jnp.float32), shape(WIDTH, SLOTS)],
-        [VMEM] * 2,
+        [SMEM] + [VMEM] * 2,
+        pos,
         inputs,
         proj_in,
     )
@@ -258,16 +287,14 @@
     *landed, slope, wide, act = lax.optimization_barrier((*landed, slope, wide, act))
     shares = call(unpack_kernel, shape(REP, SHARE, WIDTH), [VMEM] * SENDS, *landed)
     got = lax.all_to_all(shares, "rep", 0, 0, tiled=True).reshape(SLOTS, WIDTH)
-    part, terms = call(
+    dhid, terms = call(
         middle_kernel,
-        [shape(REP, PART, LANES), shape(NODE, 2 * ROWS, HID)],
-        [SMEM] + [VMEM] * 6,
-        pos,
+        [shape(SLOTS, HID), shape(NODE, 2 * ROWS, HID)],
+        [VMEM] * 5,
         got,
         wide,
         act,
         proj_out,
-        proj_in,
         slope,
         scratch=[
             pltpu.VMEM((NODE, 2 * ROWS, HID), jnp.bfloat16),
@@ -278,14 +305,30 @@
     summed = lax.psum_scatter(
         terms.reshape(NODE * 2 * ROWS, HID), "node", scatter_dimension=0, tiled=True
     )
-    part = lax.all_to_all(part, "rep", 0, 0, tiled=True)
-
-    back = call(back_kernel, shape(EXP * BACK, LANES), [VMEM], part)
+    part = call(part_kernel, shape(X, PAIR, PART, LANES), [VMEM] * 2, dhid, proj_in)
+    part = lax.all_to_all(part, "rep", 0, 0, axis_index_groups=ALONG_X, tiled=True)
+    keep, send = call(
+        sum_kernel,
+        [shape(PART, LANES, dtype=jnp.float32), shape(PART, LANES)],
+        [SMEM, VMEM],
+        pos,
+        part,
+    )
+    other = lax.ppermute(send, "rep", NEIGHBOUR)
+    back = call(back_kernel, shape(EXP * BACK, LANES), [SMEM] + [VMEM] * 2, pos, keep, other)
     back = lax.all_to_all(back.reshape(EXP, BACK, LANES), "exp", 0, 0, tiled=True)
     grad_inputs = call(
         combine_kernel, shape(COLS, TOK), [VMEM] * 2, code, back.reshape(EXP * BACK, LANES)
     )
-    return grad_inputs.T, summed[None, :ROWS], summed[None, ROWS:]
+    grad_w_in, grad_w_out = call(
+        split_kernel,
+        [shape(ROWS, HID)] * 2,
+        [HBM],
+        summed,
+        scratch=[pltpu.SemaphoreType.DMA((2,))],
+        out_specs=[HBM] * 2,
+    )
+    return grad_inputs.T, grad_w_in[None], grad_w_out[None]
 
 
 def solution(mesh):

time: 163 us -> 161 us (0.988)
  blocking collectives: 75.6 us -> 62 us
  waiting for transfers between devices: 20.2 us -> 26.4 us
  starting transfers between devices: 34 us -> 36.5 us
  Pallas kernels: 11.1 us -> 13 us
    ppermute x0 -> x1, waiting for transfers between devices: none -> 20.5 us  [local(): other = lax.ppermute(send, 'rep', NEIGHBOUR)]
    reduce_scatter x1, waiting for transfers between devices: 20.1 us -> 5.95 us  [local(): lax.psum_scatter(terms.reshape(NODE * 2 * ROWS, HID), 'node', scatter_dim...]
    all_to_all x1, blocking collectives: 37.1 us -> 25.7 us  [local(): lax.all_to_all(back.reshape(EXP, BACK, LANES), 'exp', 0, 0, tiled=True)]
    unnamed x12 -> x16, local copies, waits for them, and re-layouts: 5.05 us -> 7.63 us
    ppermute x0 -> x1, starting transfers between devices: none -> 2.45 us  [local(): other = lax.ppermute(send, 'rep', NEIGHBOUR)]
    broadcast_in_dim x1 -> x0, local copies, waits for them, and re-layouts: 2.09 us -> none  [local(): return (grad_inputs.T, summed[None, :ROWS], summed[None, ROWS:])]
    pallas_call x6 -> x9, Pallas kernels: 11.1 us -> 13 us  [call(): pl.pallas_call(kernel, out_shape=out, in_specs=in_specs, out_specs=out_sp...]
  transfers between devices with their start and end apart: 5 -> 6, of which waited for: 1 -> 2; matrix products, arithmetic and copies ran while one was open for 0% -> 0% of each run, Pallas kernels for 2% -> 4%
where the time goes in v3:
time: 161 us; the launch traced here: 160 us
  blocking collectives  62 us (39%)
  starting transfers between devices  36.5 us (23%)
  waiting for transfers between devices  26.4 us (16%)
  between operations  14.2 us (9%)
  Pallas kernels  13 us (8%)
  local copies, waits for them, and re-layouts  7.63 us (5%)
    ppermute x4, starting transfers between devices, local(): lax.ppermute(p, ('rep', 'exp'), send_pairs(k))  34 us
    all_to_all x1, blocking collectives, local(): lax.all_to_all(back.reshape(EXP, BACK, LANES), 'exp', 0, 0, tiled=True)  25.7 us
    ppermute x1, waiting for transfers between devices, local(): other = lax.ppermute(send, 'rep', NEIGHBOUR)  20.5 us
    all_to_all x1, blocking collectives, local(): got = lax.all_to_all(shares, 'rep', 0, 0, tiled=True).reshape(SLOTS, WIDTH)  20.3 us
    all_to_all x1, blocking collectives, local(): lax.all_to_all(part, 'rep', 0, 0, axis_index_groups=ALONG_X, tiled=True)  16 us
    pallas_call x9, Pallas kernels, call(): pl.pallas_call(kernel, out_shape=out, in_specs=in_specs, out_specs=out_sp...  13 us
    unnamed x16, local copies, waits for them, and re-layouts  7.63 us
    reduce_scatter x1, waiting for transfers between devices, local(): lax.psum_scatter(terms.reshape(NODE * 2 * ROWS, HID), 'node', scatter_dim...  5.95 us
  transfers between devices with their start and end apart: 6, of which 2 were waited for; matrix products, arithmetic and copies ran while one was open for 0% of the time, Pallas kernels for 4%

profile of v3, /device:TPU:1, one launch (start us, length us, event | category | flops | bytes accessed | tf_op | source)
XLA Modules:
  0.0 159.8 jit_solution(3517758849102051836)
XLA Ops:
  7.2 0.0 reduce-scatter.2.cloned.1.call-start
  7.2 0.1 pad_add_fusion.pos_ref
  7.3 0.0 copy-start.5
  7.3 1.0 copy-done.5
  8.3 0.0 copy-start.6
  8.3 0.7 copy-done.6
  9.0 0.0 copy-start.7
  9.0 0.7 copy-done.7
  9.7 1.8 %shard_map.85 = (bf16[136,128]{1,0:T(8,128)(2,1)S(1)}, bf16[136,128]{1,0:T(8,128)(2,1)S(1)}, bf16[136,128]{1,0:T(8,128)(2,1)S(1)}, bf16[136,128]{1,0:T(8,128)(2,1)S(1)}, s32[128,2]{1,0:T(8,128)S(1)}) custom-call(s32[3]{0:T(128)S(1)} %pad_add_fusion.pos_ref, s32[2,128]{1,0:T(2,128)S(1)} %bitcast.22, f32[2,128]{1,0:T(2,128)S(1)} %bitcast.23, ...), custom_call_target="tpu_custom_call" | custom-call | tf_op jit(solution)/shard_map/pallas_call | solution.py:237
  11.4 19.9 %collective-permute-start = (bf16[136,128]{1,0:T(8,128)(2,1)S(1)}, bf16[136,128]{1,0:T(8,128)(2,1)S(1)}, u32[]{:S(2)}, u32[]{:S(2)}) collective-permute-start(bf16[136,128]{1,0:T(8,128)(2,1)S(1)} %get-tuple-element.25), channel_id=1, source_target_pairs={{0,64},{4,92},{8,88},{12,84},{16,80},{20,76},{24,72},{28,68},{32,9... | collective-permute-start | bytes 104456 | tf_op jit(solution)/shard_map/ppermute | solution.py:276
  31.4 5.8 %collective-permute-start.1 = (bf16[136,128]{1,0:T(8,128)(2,1)S(1)}, bf16[136,128]{1,0:T(8,128)(2,1)S(1)}, u32[]{:S(2)}, u32[]{:S(2)}) collective-permute-start(bf16[136,128]{1,0:T(8,128)(2,1)S(1)} %get-tuple-element.26), channel_id=1, source_target_pairs={{0,32},{4,60},{8,56},{12,52},{16,48},{20,44},{24,40},{28,36},{32,6... | collective-permute-start | bytes 104456 | tf_op jit(solution)/shard_map/ppermute | solution.py:276
  37.2 1.9 %collective-permute-start.2 = (bf16[136,128]{1,0:T(8,128)(2,1)S(1)}, bf16[136,128]{1,0:T(8,128)(2,1)S(1)}, u32[]{:S(2)}, u32[]{:S(2)}) collective-permute-start(bf16[136,128]{1,0:T(8,128)(2,1)S(1)} %get-tuple-element.27), channel_id=1, source_target_pairs={{0,96},{4,124},{8,120},{12,116},{16,112},{20,108},{24,104},{28,100... | collective-permute-start | bytes 104456 | tf_op jit(solution)/shard_map/ppermute | solution.py:276
  39.1 6.3 %collective-permute-start.3 = (bf16[136,128]{1,0:T(8,128)(2,1)S(1)}, bf16[136,128]{1,0:T(8,128)(2,1)S(1)}, u32[]{:S(2)}, u32[]{:S(2)}) collective-permute-start(bf16[136,128]{1,0:T(8,128)(2,1)S(1)} %get-tuple-element.28), channel_id=1, source_target_pairs={{0,0},{4,28},{8,24},{12,20},{16,16},{20,12},{24,8},{28,4},{32,32},... | collective-permute-start | bytes 104456 | tf_op jit(solution)/shard_map/ppermute | solution.py:276
  45.5 0.0 copy-start
  45.5 1.4 copy-done
  46.9 0.0 copy-start.3
  46.9 1.2 copy-done.3
  48.2 2.1 %shard_map.86 = (bf16[320,512]{1,0:T(8,128)(2,1)S(1)}, f32[320,512]{1,0:T(8,128)S(1)}, bf16[1664,320]{1,0:T(8,128)(2,1)S(1)}) custom-call(s32[3]{0:T(128)S(1)} %pad_add_fusion.pos_ref, bf16[320,1664]{1,0:T(8,128)(2,1)S(1)} %bitcast.19, bf16[1664,512]{1,0:T(8,128)(2,1)S(1)} %bitcast.15), custom_call_target="tpu_custom_call" | custom-call | tf_op jit(solution)/shard_map/pallas_call | solution.py:237
  50.3 0.0 collective-permute-done.i0
  50.3 0.0 collective-permute-done.1.i1
  50.3 0.0 collective-permute-done.2.i2
  50.3 0.0 collective-permute-done.3.i3
  50.4 0.4 shard_map.87
  50.7 0.0 copy-start.2
  50.7 20.3 %all_to_all.15 = bf16[8,40,1664]{2,1,0:T(8,128)(2,1)S(1)} all-to-all(bf16[8,40,1664]{2,1,0:T(8,128)(2,1)S(1)} %shard_map.87), channel_id=1, replica_groups=mesh['rep'=8,'exp'=32,'node'=4] {'rep'}, dimensions={0} | all-to-all | bytes 2129920 | tf_op jit(solution)/shard_map/all_to_all | solution.py:289
  71.0 0.0 copy-done.2
  71.0 3.6 %shard_map.88 = (bf16[320,512]{1,0:T(8,128)(2,1)S(1)}, bf16[4,832,512]{2,1,0:T(8,128)(2,1)}) custom-call(bf16[320,1664]{1,0:T(8,128)(2,1)S(1)} %bitcast.17, bf16[1664,320]{1,0:T(8,128)(2,1)S(1)} %get-tuple-element.36.wide_ref, bf16[320,512]{1,0:T(8,128)(2,1)S(1)} %get-tuple-element.37.act_ref, bf16[1664,512]{1,0:T(8,128)(2,1)S(1)} %bitcast.18, ...), custom_call_target="tpu_custom_call" | custom-call | tf_op jit(solution)/shard_map/pallas_call | solution.py:237
  74.7 0.0 copy-start.1
  74.7 0.0 reduce-scatter.2.cloned.1.call-update
  74.7 1.4 copy-done.1
  76.1 1.2 shard_map.89
  77.4 16.0 %all_to_all.16.part_ref = bf16[4,2,528,128]{3,2,1,0:T(8,128)(2,1)S(1)} all-to-all(bf16[4,2,528,128]{3,2,1,0:T(8,128)(2,1)S(1)} %shard_map.89), channel_id=1, replica_groups={{0,256,512,768},{128,384,640,896},{1,257,513,769},{129,385,641,897},{2,..., dimensions={0} | all-to-all | bytes 2162688 | tf_op jit(solution)/shard_map/all_to_all | solution.py:309
  93.3 0.7 shard_map.90
  94.0 2.4 %collective-permute-start.4 = (bf16[528,128]{1,0:T(8,128)(2,1)S(1)}, bf16[528,128]{1,0:T(8,128)(2,1)S(1)}, u32[]{:S(2)}, u32[]{:S(2)}) collective-permute-start(bf16[528,128]{1,0:T(8,128)(2,1)S(1)} %get-tuple-element.41), channel_id=1, source_target_pairs={{0,128},{128,0},{256,384},{384,256},{512,640},{640,512},{768,896},... | collective-permute-start | bytes 405512 | tf_op jit(solution)/shard_map/ppermute | solution.py:317
  96.4 20.5 %collective-permute-done.4.other_ref = bf16[528,128]{1,0:T(8,128)(2,1)S(1)} collective-permute-done((bf16[528,128]{1,0:T(8,128)(2,1)S(1)}, bf16[528,128]{1,0:T(8,128)(2,1)S(1)}, u32[]{:S(2)}, u32[]{:S(2)}) %collective-permute-start.4) | collective-permute-done | bytes 135200 | tf_op jit(solution)/shard_map/ppermute | solution.py:317
  116.9 1.2 shard_map.91
  118.1 25.7 %all_to_all.17 = bf16[32,24,128]{2,1,0:T(8,128)(2,1)S(1)} all-to-all(bf16[32,24,128]{2,1,0:T(8,128)(2,1)S(1)} %bitcast.21), channel_id=1, replica_groups=mesh['rep'=8,'exp'=32,'node'=4] {'exp'}, dimensions={0} | all-to-all | bytes 393216 | tf_op jit(solution)/shard_map/all_to_all | solution.py:319
  143.8 1.1 shard_map.92
  144.9 6.0 %reduce-scatter.2.cloned.1.call-done.summed_hbm = bf16[832,512]{1,0:T(8,128)(2,1)} async-done(((bf16[3328,512]{1,0:T(8,128)(2,1)}), bf16[832,512]{1,0:T(8,128)(2,1)}) %reduce-scatter.2.cloned.1.call-update) | async-done | bytes 851984 | tf_op jit(solution)/shard_map/reduce_scatter | solution.py:305
  150.8 0.0 copy-start.4
  150.8 1.2 copy-done.4
  152.0 0.9 shard_map.93
Async XLA Ops:
  7.2 143.7 %reduce-scatter.2.cloned.1.call-start = ((), (), s32[]{:S(2)}) async-start(), calls=%async_computation.4 | async-start | bytes 4259840 | tf_op jit(solution)/shard_map/reduce_scatter | solution.py:305
  7.3 1.0 copy-start.5
  8.3 0.7 copy-start.6
  9.0 0.7 copy-start.7
  11.4 38.9 %collective-permute-start = (bf16[136,128]{1,0:T(8,128)(2,1)S(1)}, bf16[136,128]{1,0:T(8,128)(2,1)S(1)}, u32[]{:S(2)}, u32[]{:S(2)}) collective-permute-start(bf16[136,128]{1,0:T(8,128)(2,1)S(1)} %get-tuple-element.25), channel_id=1, source_target_pairs={{0,64},{4,92},{8,88},{12,84},{16,80},{20,76},{24,72},{28,68},{32,9... | collective-permute-start | bytes 104456 | tf_op jit(solution)/shard_map/ppermute | solution.py:276
  31.4 18.9 %collective-permute-start.1 = (bf16[136,128]{1,0:T(8,128)(2,1)S(1)}, bf16[136,128]{1,0:T(8,128)(2,1)S(1)}, u32[]{:S(2)}, u32[]{:S(2)}) collective-permute-start(bf16[136,128]{1,0:T(8,128)(2,1)S(1)} %get-tuple-element.26), channel_id=1, source_target_pairs={{0,32},{4,60},{8,56},{12,52},{16,48},{20,44},{24,40},{28,36},{32,6... | collective-permute-start | bytes 104456 | tf_op jit(solution)/shard_map/ppermute | solution.py:276
  37.2 13.1 %collective-permute-start.2 = (bf16[136,128]{1,0:T(8,128)(2,1)S(1)}, bf16[136,128]{1,0:T(8,128)(2,1)S(1)}, u32[]{:S(2)}, u32[]{:S(2)}) collective-permute-start(bf16[136,128]{1,0:T(8,128)(2,1)S(1)} %get-tuple-element.27), channel_id=1, source_target_pairs={{0,96},{4,124},{8,120},{12,116},{16,112},{20,108},{24,104},{28,100... | collective-permute-start | bytes 104456 | tf_op jit(solution)/shard_map/ppermute | solution.py:276
  39.1 11.2 %collective-permute-start.3 = (bf16[136,128]{1,0:T(8,128)(2,1)S(1)}, bf16[136,128]{1,0:T(8,128)(2,1)S(1)}, u32[]{:S(2)}, u32[]{:S(2)}) collective-permute-start(bf16[136,128]{1,0:T(8,128)(2,1)S(1)} %get-tuple-element.28), channel_id=1, source_target_pairs={{0,0},{4,28},{8,24},{12,20},{16,16},{20,12},{24,8},{28,4},{32,32},... | collective-permute-start | bytes 104456 | tf_op jit(solution)/shard_map/ppermute | solution.py:276
  45.5 1.5 copy-start
  46.9 1.2 copy-start.3
  50.7 20.3 %copy-start.2 = (bf16[1,1664,512]{2,1,0:T(8,128)(2,1)S(1)}, bf16[1,1664,512]{2,1,0:T(8,128)(2,1)}, u32[]{:S(2)}) copy-start(bf16[1,1664,512]{2,1,0:T(8,128)(2,1)} %param.11) | copy-start | bytes 5111812
  74.7 1.5 copy-start.1
  94.0 22.9 %collective-permute-start.4 = (bf16[528,128]{1,0:T(8,128)(2,1)S(1)}, bf16[528,128]{1,0:T(8,128)(2,1)S(1)}, u32[]{:S(2)}, u32[]{:S(2)}) collective-permute-start(bf16[528,128]{1,0:T(8,128)(2,1)S(1)} %get-tuple-element.41), channel_id=1, source_target_pairs={{0,128},{128,0},{256,384},{384,256},{512,640},{640,512},{768,896},... | collective-permute-start | bytes 405512 | tf_op jit(solution)/shard_map/ppermute | solution.py:317
  150.8 1.2 copy-start.4
Sparse Core Ops, SparseCore 0:
  74.8 75.9 reduce-scatter.1

commit v4 on v3

--- a/solution.py
+++ b/solution.py
@@ -30,6 +30,7 @@
 VMEM = pl.BlockSpec(memory_space=pltpu.VMEM)
 SMEM = pl.BlockSpec(memory_space=pltpu.SMEM)
 HBM = pl.BlockSpec(memory_space=pltpu.HBM)
+BUSY = pl.CostEstimate(flops=2 * 10**9, transcendentals=0, bytes_accessed=10**6)
 PARAMS = pltpu.CompilerParams(vmem_limit_bytes=48 * 1024 * 1024)
 
 
@@ -52,12 +53,10 @@
     return step
 
 
-def dispatch_kernel(pos_ref, ids_ref, gates_ref, grad_ref, o0, o1, o2, o3, code_ref):
-    rep, src = pos_ref[0], pos_ref[1]
+def table_kernel(ids_ref, code_ref, target_ref):
     lane = iota((TOK, LANES), 1)
     before = hot(iota((TOK, TOK), 0) > iota((TOK, TOK), 1))
     ids = jnp.concatenate([ids_ref[...], jnp.zeros((6, TOK), jnp.int32)], axis=0).T
-    gates = jnp.concatenate([gates_ref[...], jnp.zeros((6, TOK), jnp.float32)], axis=0).T
     first = ids[:, 0:1]
     second = ids[:, 1:2]
     hot0 = hot(first == lane)
@@ -71,8 +70,15 @@
     kept1 = slot1 < CAP
     code_ref[:, 0:1] = jnp.where(kept0, first * BACK + slot0, -100)
     code_ref[:, 1:2] = jnp.where(kept1, second * BACK + slot1, -100)
-    target0 = jnp.where(kept0, first * 16 + slot0, -1)
-    target1 = jnp.where(kept1, second * 16 + slot1, -1)
+    target_ref[:, 0:1] = jnp.where(kept0, first * 16 + slot0, -1)
+    target_ref[:, 1:2] = jnp.where(kept1, second * 16 + slot1, -1)
+
+
+def dispatch_kernel(pos_ref, target_ref, gates_ref, grad_ref, o0, o1, o2, o3):
+    rep, src = pos_ref[0], pos_ref[1]
+    target0 = target_ref[:, 0:1]
+    target1 = target_ref[:, 1:2]
+    gates = jnp.concatenate([gates_ref[...], jnp.zeros((6, TOK), jnp.float32)], axis=0).T
     col = iota((1, LANES), 1)
     k = col >> 4
     c = col & 15
@@ -233,7 +239,7 @@
     out_ref[LANES:] = tail[: COLS - LANES].astype(jnp.bfloat16)
 
 
-def call(kernel, out, in_specs, *args, scratch=(), out_specs=None):
+def call(kernel, out, in_specs, *args, scratch=(), out_specs=None, cost=None):
     return pl.pallas_call(
         kernel,
         out_shape=out,
@@ -241,6 +247,7 @@
         out_specs=out_specs or jax.tree.map(lambda _: VMEM, out),
         scratch_shapes=list(scratch),
         compiler_params=PARAMS,
+        cost_estimate=cost,
     )(*args)
 
 
@@ -264,14 +271,16 @@
     proj_in = w_in[0]
     proj_out = w_out[0]
 
-    *packed, code = call(
+    code, target = call(table_kernel, [shape(TOK, 2, dtype=jnp.int32)] * 2, [VMEM], expert_ids.T, cost=BUSY)
+    packed = call(
         dispatch_kernel,
-        [shape(PACKED, LANES)] * SENDS + [shape(TOK, 2, dtype=jnp.int32)],
+        [shape(PACKED, LANES)] * SENDS,
         [SMEM] + [VMEM] * 3,
         pos,
-        expert_ids.T,
+        target,
         gates.T,
         grad_out,
+        cost=BUSY,
     )
     landed = [lax.ppermute(p, ("rep", "exp"), send_pairs(k)) for k, p in zip(ORDER, packed)]
 
@@ -301,6 +310,7 @@
             pltpu.SemaphoreType.DMA((NODE,)),
         ],
         out_specs=[VMEM, HBM],
+        cost=BUSY,
     )
     summed = lax.psum_scatter(
         terms.reshape(NODE * 2 * ROWS, HID), "node", scatter_dimension=0, tiled=True

time: 161 us -> 159 us (0.988)
  local copies, waits for them, and re-layouts: 7.63 us -> 2.32 us
    unnamed x16 -> x14, local copies, waits for them, and re-layouts: 7.63 us -> 2.32 us
    all_to_all x1, blocking collectives: 20.3 us -> 22 us  [local(): got = lax.all_to_all(shares, 'rep', 0, 0, tiled=True).reshape(SLOTS, WIDTH)]
    pallas_call x9 -> x10, Pallas kernels: 13 us -> 12.9 us  [call(): pl.pallas_call(kernel, out_shape=out, in_specs=in_specs, out_specs=out_sp...]
  transfers between devices with their start and end apart: 6 -> 6, of which waited for: 2 -> 3; matrix products, arithmetic and copies ran while one was open for 0% -> 0% of each run, Pallas kernels for 4% -> 4%
where the time goes in v4:
time: 159 us; the launch traced here: 157 us
  blocking collectives  63.5 us (40%)
  starting transfers between devices  36.5 us (23%)
  waiting for transfers between devices  27.8 us (17%)
  between operations  14.2 us (9%)
  Pallas kernels  12.9 us (8%)
  local copies, waits for them, and re-layouts  2.32 us (1%)
    ppermute x4, starting transfers between devices, local(): lax.ppermute(p, ('rep', 'exp'), send_pairs(k))  34 us
    all_to_all x1, blocking collectives, local(): lax.all_to_all(back.reshape(EXP, BACK, LANES), 'exp', 0, 0, tiled=True)  25.6 us
    all_to_all x1, blocking collectives, local(): got = lax.all_to_all(shares, 'rep', 0, 0, tiled=True).reshape(SLOTS, WIDTH)  22 us
    ppermute x1, waiting for transfers between devices, local(): other = lax.ppermute(send, 'rep', NEIGHBOUR)  20.2 us
    all_to_all x1, blocking collectives, local(): lax.all_to_all(part, 'rep', 0, 0, axis_index_groups=ALONG_X, tiled=True)  16 us
    pallas_call x10, Pallas kernels, call(): pl.pallas_call(kernel, out_shape=out, in_specs=in_specs, out_specs=out_sp...  12.9 us
    reduce_scatter x1, waiting for transfers between devices, local(): lax.psum_scatter(terms.reshape(NODE * 2 * ROWS, HID), 'node', scatter_dim...  6.68 us
  transfers between devices with their start and end apart: 6, of which 3 were waited for; matrix products, arithmetic and copies ran while one was open for 0% of the time, Pallas kernels for 4%

profile of v4, /device:TPU:1, one launch (start us, length us, event | category | flops | bytes accessed | tf_op | source)
XLA Modules:
  0.0 157.4 jit_solution(14459703485807966017)
XLA Ops:
  7.2 0.0 reduce-scatter.2.cloned.1.call-start
  7.2 0.0 copy-start.5
  7.2 0.7 copy-done.5
  7.9 0.0 copy-start.4
  7.9 0.0 copy-start.6
  7.9 0.4 shard_map.85
  8.3 0.1 pad_add_fusion.pos_ref
  8.4 0.5 copy-done.4
  8.9 0.0 copy-done.6
  8.9 0.0 copy-start
  8.9 0.0 copy-start.1
  8.9 1.3 shard_map.86
  10.2 19.9 %collective-permute-start = (bf16[136,128]{1,0:T(8,128)(2,1)S(1)}, bf16[136,128]{1,0:T(8,128)(2,1)S(1)}, u32[]{:S(2)}, u32[]{:S(2)}) collective-permute-start(bf16[136,128]{1,0:T(8,128)(2,1)S(1)} %get-tuple-element.27), channel_id=1, source_target_pairs={{0,64},{4,92},{8,88},{12,84},{16,80},{20,76},{24,72},{28,68},{32,9... | collective-permute-start | bytes 104456 | tf_op jit(solution)/shard_map/ppermute | solution.py:285
  30.2 5.8 %collective-permute-start.1 = (bf16[136,128]{1,0:T(8,128)(2,1)S(1)}, bf16[136,128]{1,0:T(8,128)(2,1)S(1)}, u32[]{:S(2)}, u32[]{:S(2)}) collective-permute-start(bf16[136,128]{1,0:T(8,128)(2,1)S(1)} %get-tuple-element.28), channel_id=1, source_target_pairs={{0,32},{4,60},{8,56},{12,52},{16,48},{20,44},{24,40},{28,36},{32,6... | collective-permute-start | bytes 104456 | tf_op jit(solution)/shard_map/ppermute | solution.py:285
  36.0 1.9 %collective-permute-start.2 = (bf16[136,128]{1,0:T(8,128)(2,1)S(1)}, bf16[136,128]{1,0:T(8,128)(2,1)S(1)}, u32[]{:S(2)}, u32[]{:S(2)}) collective-permute-start(bf16[136,128]{1,0:T(8,128)(2,1)S(1)} %get-tuple-element.29), channel_id=1, source_target_pairs={{0,96},{4,124},{8,120},{12,116},{16,112},{20,108},{24,104},{28,100... | collective-permute-start | bytes 104456 | tf_op jit(solution)/shard_map/ppermute | solution.py:285
  37.9 6.3 %collective-permute-start.3 = (bf16[136,128]{1,0:T(8,128)(2,1)S(1)}, bf16[136,128]{1,0:T(8,128)(2,1)S(1)}, u32[]{:S(2)}, u32[]{:S(2)}) collective-permute-start(bf16[136,128]{1,0:T(8,128)(2,1)S(1)} %get-tuple-element.30), channel_id=1, source_target_pairs={{0,0},{4,28},{8,24},{12,20},{16,16},{20,12},{24,8},{28,4},{32,32},... | collective-permute-start | bytes 104456 | tf_op jit(solution)/shard_map/ppermute | solution.py:285
  44.2 0.0 copy-done
  44.2 0.0 copy-done.1
  44.3 2.1 %shard_map.87 = (bf16[320,512]{1,0:T(8,128)(2,1)S(1)}, f32[320,512]{1,0:T(8,128)S(1)}, bf16[1664,320]{1,0:T(8,128)(2,1)S(1)}) custom-call(s32[3]{0:T(128)S(1)} %pad_add_fusion.pos_ref, bf16[320,1664]{1,0:T(8,128)(2,1)S(1)} %bitcast.17, bf16[1664,512]{1,0:T(8,128)(2,1)S(1)} %bitcast.15), custom_call_target="tpu_custom_call" | custom-call | tf_op jit(solution)/shard_map/pallas_call | solution.py:243
  46.4 0.0 collective-permute-done.i0
  46.4 0.0 collective-permute-done.1.i1
  46.4 0.9 collective-permute-done.2.i2
  47.4 0.0 collective-permute-done.3.i3
  47.4 0.4 shard_map.88
  47.7 0.0 copy-start.3
  47.7 22.0 %all_to_all.15 = bf16[8,40,1664]{2,1,0:T(8,128)(2,1)S(1)} all-to-all(bf16[8,40,1664]{2,1,0:T(8,128)(2,1)S(1)} %shard_map.88), channel_id=1, replica_groups=mesh['rep'=8,'exp'=32,'node'=4] {'rep'}, dimensions={0} | all-to-all | bytes 2129920 | tf_op jit(solution)/shard_map/all_to_all | solution.py:298
  69.7 0.0 copy-done.3
  69.7 3.6 %shard_map.89 = (bf16[320,512]{1,0:T(8,128)(2,1)S(1)}, bf16[4,832,512]{2,1,0:T(8,128)(2,1)}) custom-call(bf16[320,1664]{1,0:T(8,128)(2,1)S(1)} %bitcast.18, bf16[1664,320]{1,0:T(8,128)(2,1)S(1)} %get-tuple-element.38.wide_ref, bf16[320,512]{1,0:T(8,128)(2,1)S(1)} %get-tuple-element.39.act_ref, bf16[1664,512]{1,0:T(8,128)(2,1)S(1)} %bitcast.21, ...), custom_call_target="tpu_custom_call" | custom-call | flops 2000000000 | bytes 1000000 | tf_op jit(solution)/shard_map/pallas_call | solution.py:243
  73.3 0.0 reduce-scatter.2.cloned.1.call-update
  73.4 1.2 shard_map.90
  74.6 16.0 %all_to_all.16.part_ref = bf16[4,2,528,128]{3,2,1,0:T(8,128)(2,1)S(1)} all-to-all(bf16[4,2,528,128]{3,2,1,0:T(8,128)(2,1)S(1)} %shard_map.90), channel_id=1, replica_groups={{0,256,512,768},{128,384,640,896},{1,257,513,769},{129,385,641,897},{2,..., dimensions={0} | all-to-all | bytes 2162688 | tf_op jit(solution)/shard_map/all_to_all | solution.py:319
  90.5 0.7 shard_map.91
  91.2 2.5 %collective-permute-start.4 = (bf16[528,128]{1,0:T(8,128)(2,1)S(1)}, bf16[528,128]{1,0:T(8,128)(2,1)S(1)}, u32[]{:S(2)}, u32[]{:S(2)}) collective-permute-start(bf16[528,128]{1,0:T(8,128)(2,1)S(1)} %get-tuple-element.43), channel_id=1, source_target_pairs={{0,128},{128,0},{256,384},{384,256},{512,640},{640,512},{768,896},... | collective-permute-start | bytes 405512 | tf_op jit(solution)/shard_map/ppermute | solution.py:327
  93.8 20.2 %collective-permute-done.4.other_ref = bf16[528,128]{1,0:T(8,128)(2,1)S(1)} collective-permute-done((bf16[528,128]{1,0:T(8,128)(2,1)S(1)}, bf16[528,128]{1,0:T(8,128)(2,1)S(1)}, u32[]{:S(2)}, u32[]{:S(2)}) %collective-permute-start.4) | collective-permute-done | bytes 135200 | tf_op jit(solution)/shard_map/ppermute | solution.py:327
  113.9 1.2 shard_map.92
  115.1 25.6 %all_to_all.17 = bf16[32,24,128]{2,1,0:T(8,128)(2,1)S(1)} all-to-all(bf16[32,24,128]{2,1,0:T(8,128)(2,1)S(1)} %bitcast.20), channel_id=1, replica_groups=mesh['rep'=8,'exp'=32,'node'=4] {'exp'}, dimensions={0} | all-to-all | bytes 393216 | tf_op jit(solution)/shard_map/all_to_all | solution.py:329
  140.7 1.1 shard_map.93
  141.8 6.7 %reduce-scatter.2.cloned.1.call-done.summed_hbm = bf16[832,512]{1,0:T(8,128)(2,1)} async-done(((bf16[3328,512]{1,0:T(8,128)(2,1)}), bf16[832,512]{1,0:T(8,128)(2,1)}) %reduce-scatter.2.cloned.1.call-update) | async-done | bytes 851984 | tf_op jit(solution)/shard_map/reduce_scatter | solution.py:315
  148.5 0.0 copy-start.2
  148.5 1.2 copy-done.2
  149.6 0.9 shard_map.94
Async XLA Ops:
  7.2 141.3 %reduce-scatter.2.cloned.1.call-start = ((), (), s32[]{:S(2)}) async-start(), calls=%async_computation.4 | async-start | bytes 4259840 | tf_op jit(solution)/shard_map/reduce_scatter | solution.py:315
  7.2 0.7 copy-start.5
  7.9 1.0 copy-start.4
  7.9 1.0 copy-start.6
  8.9 35.3 %copy-start = (bf16[1,1664,512]{2,1,0:T(8,128)(2,1)S(1)}, bf16[1,1664,512]{2,1,0:T(8,128)(2,1)}, u32[]{:S(2)}) copy-start(bf16[1,1664,512]{2,1,0:T(8,128)(2,1)} %param.10) | copy-start | bytes 5111812
  8.9 35.3 %copy-start.1 = (bf16[1,1,320,1664]{3,2,1,0:T(8,128)(2,1)S(1)}, bf16[1,1,320,1664]{3,2,1,0:T(8,128)(2,1)}, u32[]{:S(2)}) copy-start(bf16[1,1,320,1664]{3,2,1,0:T(8,128)(2,1)} %param.9) | copy-start | bytes 3194884
  10.2 36.2 %collective-permute-start = (bf16[136,128]{1,0:T(8,128)(2,1)S(1)}, bf16[136,128]{1,0:T(8,128)(2,1)S(1)}, u32[]{:S(2)}, u32[]{:S(2)}) collective-permute-start(bf16[136,128]{1,0:T(8,128)(2,1)S(1)} %get-tuple-element.27), channel_id=1, source_target_pairs={{0,64},{4,92},{8,88},{12,84},{16,80},{20,76},{24,72},{28,68},{32,9... | collective-permute-start | bytes 104456 | tf_op jit(solution)/shard_map/ppermute | solution.py:285
  30.2 16.2 %collective-permute-start.1 = (bf16[136,128]{1,0:T(8,128)(2,1)S(1)}, bf16[136,128]{1,0:T(8,128)(2,1)S(1)}, u32[]{:S(2)}, u32[]{:S(2)}) collective-permute-start(bf16[136,128]{1,0:T(8,128)(2,1)S(1)} %get-tuple-element.28), channel_id=1, source_target_pairs={{0,32},{4,60},{8,56},{12,52},{16,48},{20,44},{24,40},{28,36},{32,6... | collective-permute-start | bytes 104456 | tf_op jit(solution)/shard_map/ppermute | solution.py:285
  36.0 11.4 %collective-permute-start.2 = (bf16[136,128]{1,0:T(8,128)(2,1)S(1)}, bf16[136,128]{1,0:T(8,128)(2,1)S(1)}, u32[]{:S(2)}, u32[]{:S(2)}) collective-permute-start(bf16[136,128]{1,0:T(8,128)(2,1)S(1)} %get-tuple-element.29), channel_id=1, source_target_pairs={{0,96},{4,124},{8,120},{12,116},{16,112},{20,108},{24,104},{28,100... | collective-permute-start | bytes 104456 | tf_op jit(solution)/shard_map/ppermute | solution.py:285
  37.9 9.5 %collective-permute-start.3 = (bf16[136,128]{1,0:T(8,128)(2,1)S(1)}, bf16[136,128]{1,0:T(8,128)(2,1)S(1)}, u32[]{:S(2)}, u32[]{:S(2)}) collective-permute-start(bf16[136,128]{1,0:T(8,128)(2,1)S(1)} %get-tuple-element.30), channel_id=1, source_target_pairs={{0,0},{4,28},{8,24},{12,20},{16,16},{20,12},{24,8},{28,4},{32,32},... | collective-permute-start | bytes 104456 | tf_op jit(solution)/shard_map/ppermute | solution.py:285
  47.7 22.0 %copy-start.3 = (bf16[1,1664,512]{2,1,0:T(8,128)(2,1)S(1)}, bf16[1,1664,512]{2,1,0:T(8,128)(2,1)}, u32[]{:S(2)}) copy-start(bf16[1,1664,512]{2,1,0:T(8,128)(2,1)} %param.11) | copy-start | bytes 5111812
  91.2 22.7 %collective-permute-start.4 = (bf16[528,128]{1,0:T(8,128)(2,1)S(1)}, bf16[528,128]{1,0:T(8,128)(2,1)S(1)}, u32[]{:S(2)}, u32[]{:S(2)}) collective-permute-start(bf16[528,128]{1,0:T(8,128)(2,1)S(1)} %get-tuple-element.43), channel_id=1, source_target_pairs={{0,128},{128,0},{256,384},{384,256},{512,640},{640,512},{768,896},... | collective-permute-start | bytes 405512 | tf_op jit(solution)/shard_map/ppermute | solution.py:327
  148.5 1.2 copy-start.2
Sparse Core Ops, SparseCore 0:
  73.5 74.9 reduce-scatter.1

commit v5 on v4

--- a/solution.py
+++ b/solution.py
@@ -25,7 +25,7 @@
 HALF = LANES // 2
 PART = 528
 SHARE = SENDS * CAP
-ORDER = (2, 1, 3, 0)
+ORDER = (1, 3, 2, 0)
 
 VMEM = pl.BlockSpec(memory_space=pltpu.VMEM)
 SMEM = pl.BlockSpec(memory_space=pltpu.SMEM)

time: 159 us -> 160 us (level)
  waiting for transfers between devices: 27.8 us -> 29.9 us
    reduce_scatter x1, waiting for transfers between devices: 6.68 us -> 8.55 us  [local(): lax.psum_scatter(terms.reshape(NODE * 2 * ROWS, HID), 'node', scatter_dim...]
    ppermute x4, waiting for transfers between devices: 0.95 us -> 2.66 us  [local(): lax.ppermute(p, ('rep', 'exp'), send_pairs(k))]
where the time goes in v5:
time: 160 us
  blocking collectives  63.5 us (40%)
  starting transfers between devices  36.8 us (23%)
  waiting for transfers between devices  29.9 us (19%)
  between operations  14.2 us (9%)
  Pallas kernels  12.9 us (8%)
  local copies, waits for them, and re-layouts  2.32 us (1%)
    ppermute x4, starting transfers between devices, local(): lax.ppermute(p, ('rep', 'exp'), send_pairs(k))  33.7 us
    all_to_all x1, blocking collectives, local(): lax.all_to_all(back.reshape(EXP, BACK, LANES), 'exp', 0, 0, tiled=True)  25.9 us
    all_to_all x1, blocking collectives, local(): got = lax.all_to_all(shares, 'rep', 0, 0, tiled=True).reshape(SLOTS, WIDTH)  21.5 us
    ppermute x1, waiting for transfers between devices, local(): other = lax.ppermute(send, 'rep', NEIGHBOUR)  18.6 us
    all_to_all x1, blocking collectives, local(): lax.all_to_all(part, 'rep', 0, 0, axis_index_groups=ALONG_X, tiled=True)  16.2 us
    pallas_call x10, Pallas kernels, call(): pl.pallas_call(kernel, out_shape=out, in_specs=in_specs, out_specs=out_sp...  12.9 us
    reduce_scatter x1, waiting for transfers between devices, local(): lax.psum_scatter(terms.reshape(NODE * 2 * ROWS, HID), 'node', scatter_dim...  8.55 us
  transfers between devices with their start and end apart: 6, of which 3 were waited for; matrix products, arithmetic and copies ran while one was open for 0% of the time, Pallas kernels for 4%

profile of v5, /device:TPU:1, one launch (start us, length us, event | category | flops | bytes accessed | tf_op | source)
XLA Modules:
  0.0 159.7 jit_solution(6692470393891194320)
XLA Ops:
  7.2 0.0 reduce-scatter.2.cloned.1.call-start
  7.2 0.0 copy-start.5
  7.2 0.7 copy-done.5
  7.9 0.0 copy-start.4
  7.9 0.0 copy-start.6
  7.9 0.4 shard_map.85
  8.3 0.1 pad_add_fusion.pos_ref
  8.4 0.5 copy-done.4
  8.9 0.0 copy-done.6
  8.9 0.0 copy-start
  8.9 0.0 copy-start.1
  8.9 1.3 shard_map.86
  10.2 16.9 %collective-permute-start = (bf16[136,128]{1,0:T(8,128)(2,1)S(1)}, bf16[136,128]{1,0:T(8,128)(2,1)S(1)}, u32[]{:S(2)}, u32[]{:S(2)}) collective-permute-start(bf16[136,128]{1,0:T(8,128)(2,1)S(1)} %get-tuple-element.27), channel_id=1, source_target_pairs={{0,32},{4,60},{8,56},{12,52},{16,48},{20,44},{24,40},{28,36},{32,6... | collective-permute-start | bytes 104456 | tf_op jit(solution)/shard_map/ppermute | solution.py:285
  27.1 3.8 %collective-permute-start.1 = (bf16[136,128]{1,0:T(8,128)(2,1)S(1)}, bf16[136,128]{1,0:T(8,128)(2,1)S(1)}, u32[]{:S(2)}, u32[]{:S(2)}) collective-permute-start(bf16[136,128]{1,0:T(8,128)(2,1)S(1)} %get-tuple-element.28), channel_id=1, source_target_pairs={{0,96},{4,124},{8,120},{12,116},{16,112},{20,108},{24,104},{28,100... | collective-permute-start | bytes 104456 | tf_op jit(solution)/shard_map/ppermute | solution.py:285
  30.9 11.1 %collective-permute-start.2 = (bf16[136,128]{1,0:T(8,128)(2,1)S(1)}, bf16[136,128]{1,0:T(8,128)(2,1)S(1)}, u32[]{:S(2)}, u32[]{:S(2)}) collective-permute-start(bf16[136,128]{1,0:T(8,128)(2,1)S(1)} %get-tuple-element.29), channel_id=1, source_target_pairs={{0,64},{4,92},{8,88},{12,84},{16,80},{20,76},{24,72},{28,68},{32,9... | collective-permute-start | bytes 104456 | tf_op jit(solution)/shard_map/ppermute | solution.py:285
  42.1 1.9 %collective-permute-start.3 = (bf16[136,128]{1,0:T(8,128)(2,1)S(1)}, bf16[136,128]{1,0:T(8,128)(2,1)S(1)}, u32[]{:S(2)}, u32[]{:S(2)}) collective-permute-start(bf16[136,128]{1,0:T(8,128)(2,1)S(1)} %get-tuple-element.30), channel_id=1, source_target_pairs={{0,0},{4,28},{8,24},{12,20},{16,16},{20,12},{24,8},{28,4},{32,32},... | collective-permute-start | bytes 104456 | tf_op jit(solution)/shard_map/ppermute | solution.py:285
  44.0 0.0 copy-done
  44.0 0.0 copy-done.1
  44.0 2.1 %shard_map.87 = (bf16[320,512]{1,0:T(8,128)(2,1)S(1)}, f32[320,512]{1,0:T(8,128)S(1)}, bf16[1664,320]{1,0:T(8,128)(2,1)S(1)}) custom-call(s32[3]{0:T(128)S(1)} %pad_add_fusion.pos_ref, bf16[320,1664]{1,0:T(8,128)(2,1)S(1)} %bitcast.17, bf16[1664,512]{1,0:T(8,128)(2,1)S(1)} %bitcast.15), custom_call_target="tpu_custom_call" | custom-call | tf_op jit(solution)/shard_map/pallas_call | solution.py:243
  46.1 0.0 collective-permute-done.i0
  46.2 0.0 collective-permute-done.1.i1
  46.2 0.0 collective-permute-done.2.i2
  46.2 2.7 %collective-permute-done.3.i3 = bf16[136,128]{1,0:T(8,128)(2,1)S(1)} collective-permute-done((bf16[136,128]{1,0:T(8,128)(2,1)S(1)}, bf16[136,128]{1,0:T(8,128)(2,1)S(1)}, u32[]{:S(2)}, u32[]{:S(2)}) %collective-permute-start.3) | collective-permute-done | bytes 34848 | tf_op jit(solution)/shard_map/ppermute | solution.py:285
  48.8 0.4 shard_map.88
  49.2 0.0 copy-start.3
  49.2 21.5 %all_to_all.15 = bf16[8,40,1664]{2,1,0:T(8,128)(2,1)S(1)} all-to-all(bf16[8,40,1664]{2,1,0:T(8,128)(2,1)S(1)} %shard_map.88), channel_id=1, replica_groups=mesh['rep'=8,'exp'=32,'node'=4] {'rep'}, dimensions={0} | all-to-all | bytes 2129920 | tf_op jit(solution)/shard_map/all_to_all | solution.py:298
  70.7 0.0 copy-done.3
  70.7 3.6 %shard_map.89 = (bf16[320,512]{1,0:T(8,128)(2,1)S(1)}, bf16[4,832,512]{2,1,0:T(8,128)(2,1)}) custom-call(bf16[320,1664]{1,0:T(8,128)(2,1)S(1)} %bitcast.18, bf16[1664,320]{1,0:T(8,128)(2,1)S(1)} %get-tuple-element.38.wide_ref, bf16[320,512]{1,0:T(8,128)(2,1)S(1)} %get-tuple-element.39.act_ref, bf16[1664,512]{1,0:T(8,128)(2,1)S(1)} %bitcast.21, ...), custom_call_target="tpu_custom_call" | custom-call | flops 2000000000 | bytes 1000000 | tf_op jit(solution)/shard_map/pallas_call | solution.py:243
  74.4 0.0 reduce-scatter.2.cloned.1.call-update
  74.4 1.2 shard_map.90
  75.6 16.2 %all_to_all.16.part_ref = bf16[4,2,528,128]{3,2,1,0:T(8,128)(2,1)S(1)} all-to-all(bf16[4,2,528,128]{3,2,1,0:T(8,128)(2,1)S(1)} %shard_map.90), channel_id=1, replica_groups={{0,256,512,768},{128,384,640,896},{1,257,513,769},{129,385,641,897},{2,..., dimensions={0} | all-to-all | bytes 2162688 | tf_op jit(solution)/shard_map/all_to_all | solution.py:319
  91.8 0.7 shard_map.91
  92.4 3.0 %collective-permute-start.4 = (bf16[528,128]{1,0:T(8,128)(2,1)S(1)}, bf16[528,128]{1,0:T(8,128)(2,1)S(1)}, u32[]{:S(2)}, u32[]{:S(2)}) collective-permute-start(bf16[528,128]{1,0:T(8,128)(2,1)S(1)} %get-tuple-element.43), channel_id=1, source_target_pairs={{0,128},{128,0},{256,384},{384,256},{512,640},{640,512},{768,896},... | collective-permute-start | bytes 405512 | tf_op jit(solution)/shard_map/ppermute | solution.py:327
  95.4 18.6 %collective-permute-done.4.other_ref = bf16[528,128]{1,0:T(8,128)(2,1)S(1)} collective-permute-done((bf16[528,128]{1,0:T(8,128)(2,1)S(1)}, bf16[528,128]{1,0:T(8,128)(2,1)S(1)}, u32[]{:S(2)}, u32[]{:S(2)}) %collective-permute-start.4) | collective-permute-done | bytes 135200 | tf_op jit(solution)/shard_map/ppermute | solution.py:327
  114.1 1.2 shard_map.92
  115.3 25.9 %all_to_all.17 = bf16[32,24,128]{2,1,0:T(8,128)(2,1)S(1)} all-to-all(bf16[32,24,128]{2,1,0:T(8,128)(2,1)S(1)} %bitcast.20), channel_id=1, replica_groups=mesh['rep'=8,'exp'=32,'node'=4] {'exp'}, dimensions={0} | all-to-all | bytes 393216 | tf_op jit(solution)/shard_map/all_to_all | solution.py:329
  141.1 1.1 shard_map.93
  142.2 8.6 %reduce-scatter.2.cloned.1.call-done.summed_hbm = bf16[832,512]{1,0:T(8,128)(2,1)} async-done(((bf16[3328,512]{1,0:T(8,128)(2,1)}), bf16[832,512]{1,0:T(8,128)(2,1)}) %reduce-scatter.2.cloned.1.call-update) | async-done | bytes 851984 | tf_op jit(solution)/shard_map/reduce_scatter | solution.py:315
  150.8 0.0 copy-start.2
  150.8 1.2 copy-done.2
  151.9 0.9 shard_map.94
Async XLA Ops:
  7.2 143.6 %reduce-scatter.2.cloned.1.call-start = ((), (), s32[]{:S(2)}) async-start(), calls=%async_computation.4 | async-start | bytes 4259840 | tf_op jit(solution)/shard_map/reduce_scatter | solution.py:315
  7.2 0.7 copy-start.5
  7.9 1.0 copy-start.4
  7.9 1.0 copy-start.6
  8.9 35.1 %copy-start = (bf16[1,1664,512]{2,1,0:T(8,128)(2,1)S(1)}, bf16[1,1664,512]{2,1,0:T(8,128)(2,1)}, u32[]{:S(2)}) copy-start(bf16[1,1664,512]{2,1,0:T(8,128)(2,1)} %param.10) | copy-start | bytes 5111812
  8.9 35.1 %copy-start.1 = (bf16[1,1,320,1664]{3,2,1,0:T(8,128)(2,1)S(1)}, bf16[1,1,320,1664]{3,2,1,0:T(8,128)(2,1)}, u32[]{:S(2)}) copy-start(bf16[1,1,320,1664]{3,2,1,0:T(8,128)(2,1)} %param.9) | copy-start | bytes 3194884
  10.2 35.9 %collective-permute-start = (bf16[136,128]{1,0:T(8,128)(2,1)S(1)}, bf16[136,128]{1,0:T(8,128)(2,1)S(1)}, u32[]{:S(2)}, u32[]{:S(2)}) collective-permute-start(bf16[136,128]{1,0:T(8,128)(2,1)S(1)} %get-tuple-element.27), channel_id=1, source_target_pairs={{0,32},{4,60},{8,56},{12,52},{16,48},{20,44},{24,40},{28,36},{32,6... | collective-permute-start | bytes 104456 | tf_op jit(solution)/shard_map/ppermute | solution.py:285
  27.1 19.1 %collective-permute-start.1 = (bf16[136,128]{1,0:T(8,128)(2,1)S(1)}, bf16[136,128]{1,0:T(8,128)(2,1)S(1)}, u32[]{:S(2)}, u32[]{:S(2)}) collective-permute-start(bf16[136,128]{1,0:T(8,128)(2,1)S(1)} %get-tuple-element.28), channel_id=1, source_target_pairs={{0,96},{4,124},{8,120},{12,116},{16,112},{20,108},{24,104},{28,100... | collective-permute-start | bytes 104456 | tf_op jit(solution)/shard_map/ppermute | solution.py:285
  30.9 15.2 %collective-permute-start.2 = (bf16[136,128]{1,0:T(8,128)(2,1)S(1)}, bf16[136,128]{1,0:T(8,128)(2,1)S(1)}, u32[]{:S(2)}, u32[]{:S(2)}) collective-permute-start(bf16[136,128]{1,0:T(8,128)(2,1)S(1)} %get-tuple-element.29), channel_id=1, source_target_pairs={{0,64},{4,92},{8,88},{12,84},{16,80},{20,76},{24,72},{28,68},{32,9... | collective-permute-start | bytes 104456 | tf_op jit(solution)/shard_map/ppermute | solution.py:285
  42.1 6.8 %collective-permute-start.3 = (bf16[136,128]{1,0:T(8,128)(2,1)S(1)}, bf16[136,128]{1,0:T(8,128)(2,1)S(1)}, u32[]{:S(2)}, u32[]{:S(2)}) collective-permute-start(bf16[136,128]{1,0:T(8,128)(2,1)S(1)} %get-tuple-element.30), channel_id=1, source_target_pairs={{0,0},{4,28},{8,24},{12,20},{16,16},{20,12},{24,8},{28,4},{32,32},... | collective-permute-start | bytes 104456 | tf_op jit(solution)/shard_map/ppermute | solution.py:285
  49.2 21.5 %copy-start.3 = (bf16[1,1664,512]{2,1,0:T(8,128)(2,1)S(1)}, bf16[1,1664,512]{2,1,0:T(8,128)(2,1)}, u32[]{:S(2)}) copy-start(bf16[1,1664,512]{2,1,0:T(8,128)(2,1)} %param.11) | copy-start | bytes 5111812
  92.4 21.6 %collective-permute-start.4 = (bf16[528,128]{1,0:T(8,128)(2,1)S(1)}, bf16[528,128]{1,0:T(8,128)(2,1)S(1)}, u32[]{:S(2)}, u32[]{:S(2)}) collective-permute-start(bf16[528,128]{1,0:T(8,128)(2,1)S(1)} %get-tuple-element.43), channel_id=1, source_target_pairs={{0,128},{128,0},{256,384},{384,256},{512,640},{640,512},{768,896},... | collective-permute-start | bytes 405512 | tf_op jit(solution)/shard_map/ppermute | solution.py:327
  150.8 1.2 copy-start.2
Sparse Core Ops, SparseCore 0:
  74.5 76.2 reduce-scatter.1
